TPU v7x, 32 devices: a whole 2x2x4 slice. The times are simulated.
32 devices in a mesh: space: 16 (over z, x, core), filt: 2 (over y).
Axes of the slice: x: 2, y: 2, z: 4, core: 2. Of those that a mesh axis runs over, the one named last changes fastest.
Arguments:
- activations: bfloat16 [64, 16, 56, 128], P('filt', 'space'), may hold values from -6 to 6
- kernel: bfloat16 [64, 64, 3, 3, 3], P('filt'), may hold values from -0.15625 to 0.15625
- preact: bfloat16 [64, 16, 56, 128], P('filt', 'space'), may hold values from -6 to 6
- upstream: bfloat16 [64, 16, 56, 128], P('filt', 'space'), may hold values from -6 to 6
Outputs:
- input_grad: bfloat16 [64, 16, 56, 128], P('filt', 'space')
- kernel_grad: float32 [64, 64, 3, 3, 3], P('filt')
All inputs are finite; a program needn't handle non-finite values.
Results may differ from a plain program's by a relative error of at most 0.0015.
Values may be sent and summed in bfloat16 or wider, within the bound.
A program may use at most 128 MiB of HBM per device.

v0:
```python
import jax
import jax.numpy as jnp
from jax import lax
from jax.sharding import PartitionSpec as P


def with_halo(block, sides, width):
    for axis, dim in sides:
        count = lax.axis_size(axis)
        forward = [(i, i + 1) for i in range(count - 1)]
        backward = [(target, source) for source, target in forward]
        low = lax.ppermute(
            lax.slice_in_dim(block, block.shape[dim] - width, None, axis=dim), axis, forward
        )
        high = lax.ppermute(lax.slice_in_dim(block, 0, width, axis=dim), axis, backward)
        block = jnp.concatenate([low, block, high], axis=dim)
    return block


def pad_plane(volume):
    return jnp.pad(volume, ((0, 0), (0, 0), (1, 1), (1, 1)))


def data_grad(grad_pad, weight):
    chans = weight.shape[1]
    depth = grad_pad.shape[1] - 2
    rows = grad_pad.shape[2] - 2
    cols = grad_pad.shape[3] - 2
    total = jnp.zeros((chans, depth, rows, cols), jnp.float32)
    for depth_off in range(3):
        for row_off in range(3):
            for col_off in range(3):
                piece = grad_pad[
                    :,
                    2 - depth_off : 2 - depth_off + depth,
                    2 - row_off : 2 - row_off + rows,
                    2 - col_off : 2 - col_off + cols,
                ]
                total = total + jnp.einsum(
                    "fc,fzyx->czyx",
                    weight[:, :, depth_off, row_off, col_off],
                    piece,
                    preferred_element_type=jnp.float32,
                )
    return total


def weight_grad(grad, input_pad):
    depth, rows, cols = (grad.shape[1], grad.shape[2], grad.shape[3])
    terms = []
    for depth_off in range(3):
        for row_off in range(3):
            for col_off in range(3):
                piece = input_pad[
                    :,
                    depth_off : depth_off + depth,
                    row_off : row_off + rows,
                    col_off : col_off + cols,
                ]
                terms.append(
                    jnp.einsum("fzyx,czyx->fc", grad, piece, preferred_element_type=jnp.float32)
                )
    stacked = jnp.stack(terms, axis=-1)
    return stacked.reshape(grad.shape[0], input_pad.shape[0], 3, 3, 3)


def on_device(activations, kernel, preact, upstream):
    masked = jnp.where(preact > 0, upstream, jnp.zeros_like(upstream))
    depth = activations.shape[1]
    volume = lax.axis_size("space") * depth * activations.shape[2] * activations.shape[3]
    scale = 1.0 / jnp.sqrt(jnp.float32(volume))
    grad_halo = with_halo(masked, (("space", 1),), 1)
    every_chan = lax.all_gather(activations, "filt", axis=0, tiled=True)
    input_halo = with_halo(every_chan, (("space", 1),), 1)
    partial_grad = data_grad(pad_plane(grad_halo), kernel)
    input_grad = lax.psum_scatter(partial_grad, "filt", scatter_dimension=0, tiled=True).astype(
        jnp.bfloat16
    )
    local_terms = weight_grad(masked, pad_plane(input_halo))
    kernel_grad = lax.psum(local_terms, "space") * scale
    return (input_grad, kernel_grad)


def solution(mesh):
    in_specs = (
        P("filt", "space", None, None),
        P("filt", None, None, None, None),
        P("filt", "space", None, None),
        P("filt", "space", None, None),
    )
    out_specs = (P("filt", "space", None, None), P("filt", None, None, None, None))
    return jax.shard_map(
        on_device, mesh=mesh, in_specs=in_specs, out_specs=out_specs, check_vma=False
    )
```

profile of v0, /device:TPU:1, one launch (start us, length us, event | category | flops | bytes accessed | tf_op | source)
XLA Modules:
  0.0 200.9 jit_solution(13932866461842942485)
XLA Ops:
  8.1 1.3 compare_select_fusion
  9.4 2.0 collective-permute-start.1
  11.4 4.5 %collective-permute-start = (bf16[32,1,56,128]{3,0,2,1:T(8,128)(2,1)S(1)}, bf16[32,1,56,128]{3,0,2,1:T(8,128)(2,1)S(1)}, u32[]{:S(2)}, u32[]{:S(2)}) collective-permute-start(bf16[32,1,56,128]{3,0,2,1:T(8,128)(2,1)S(1)} %compare_select_fusion), channel_id=1, source_target_pairs={{0,2},{2,4},{4,6},{6,8},{8,10},{10,12},{12,14},{14,16},{16,18},{18... | collective-permute-start | bytes 1376264 | tf_op jit(solution)/shard_map/ppermute | solution.py:12
  15.8 1.1 copy.8
  16.9 12.3 %all_gather.3 = bf16[64,1,56,128]{3,0,2,1:T(8,128)(2,1)S(1)} all-gather(bf16[32,1,56,128]{3,0,2,1:T(8,128)(2,1)S(1)} %copy.8), channel_id=1, replica_groups=mesh['space'=16,'filt'=2] {'filt'}, dimensions={0}, use_global_device_ids=true | all-gather | bytes 1376256 | tf_op jit(solution)/shard_map/all_gather | solution.py:73
  29.2 2.0 %collective-permute-start.3 = (bf16[64,1,56,128]{3,0,2,1:T(8,128)(2,1)S(1)}, bf16[64,1,56,128]{3,0,2,1:T(8,128)(2,1)S(1)}, u32[]{:S(2)}, u32[]{:S(2)}) collective-permute-start(bf16[64,1,56,128]{3,0,2,1:T(8,128)(2,1)S(1)} %all_gather.3), channel_id=1, source_target_pairs={{2,0},{4,2},{6,4},{8,6},{10,8},{12,10},{14,12},{16,14},{18,16},{20... | collective-permute-start | bytes 2752520 | tf_op jit(solution)/shard_map/ppermute | solution.py:15
  31.3 3.5 %collective-permute-start.2 = (bf16[64,1,56,128]{3,0,2,1:T(8,128)(2,1)S(1)}, bf16[64,1,56,128]{3,0,2,1:T(8,128)(2,1)S(1)}, u32[]{:S(2)}, u32[]{:S(2)}) collective-permute-start(bf16[64,1,56,128]{3,0,2,1:T(8,128)(2,1)S(1)} %all_gather.3), channel_id=1, source_target_pairs={{0,2},{2,4},{4,6},{6,8},{8,10},{10,12},{12,14},{14,16},{16,18},{18... | collective-permute-start | bytes 2752520 | tf_op jit(solution)/shard_map/ppermute | solution.py:12
  34.8 1.7 fusion.68
  36.5 1.9 select_maximum_fusion.2
  38.5 1.7 fusion.16
  40.2 1.7 fusion.17
  41.9 1.7 fusion.18
  43.6 1.8 fusion.19
  45.4 1.7 fusion.20
  47.1 1.7 fusion.21
  48.8 1.7 fusion.22
  50.5 1.7 fusion.23
  52.2 1.7 fusion.24
  53.9 1.7 fusion.25
  55.6 1.7 fusion.26
  57.3 1.7 fusion.27
  59.1 1.8 fusion.28
  60.8 1.8 fusion.29
  62.6 1.7 fusion.30
  64.3 1.7 fusion.31
  66.0 1.7 fusion.32
  67.7 1.7 fusion.33
  69.5 1.7 fusion.34
  71.1 1.7 fusion.35
  72.8 1.7 fusion.36
  74.5 1.7 fusion.38
  76.3 1.7 fusion.37
  78.0 1.7 fusion.39
  79.7 1.8 fusion.70
  81.5 3.9 %select_maximum_fusion = bf16[64,3,58,130]{3,0,2,1:T(8,128)(2,1)S(1)} fusion(bf16[64,1,56,128]{3,0,2,1:T(8,128)(2,1)S(1)} %collective-permute-done.3, bf16[64,1,56,128]{3,0,2,1:T(8,128)(2,1)S(1)} %all_gather.3, bf16[64,1,56,128]{3,0,2,1:T(8,128)(2,1)S(1)} %collective-permute-done.2), kind=kLoop, calls=%fused_computation.11 | loop fusion | flops 27505920 | bytes 5647872 | tf_op jit(solution)/shard_map/concatenate | solution.py:16
  85.8 0.5 convolution_dynamic-update-slice_fusion.25
  86.2 0.5 convolution_dynamic-update-slice_fusion.24
  86.7 0.4 convolution_dynamic-update-slice_fusion.23
  87.5 0.5 convolution_dynamic-update-slice_fusion.21
  87.9 0.4 convolution_dynamic-update-slice_fusion.20
  88.3 0.5 convolution_dynamic-update-slice_fusion.19
  88.8 0.5 convolution_dynamic-update-slice_fusion.18
  89.3 0.4 convolution_dynamic-update-slice_fusion.17
  89.7 0.5 convolution_dynamic-update-slice_fusion.16
  90.1 0.5 convolution_dynamic-update-slice_fusion.15
  90.6 0.4 convolution_dynamic-update-slice_fusion.14
  91.4 0.5 convolution_dynamic-update-slice_fusion.12
  91.8 0.4 convolution_dynamic-update-slice_fusion.11
  92.2 0.5 convolution_dynamic-update-slice_fusion.10
  92.7 0.5 convolution_dynamic-update-slice_fusion.9
  93.2 0.4 convolution_dynamic-update-slice_fusion.8
  93.6 0.5 convolution_dynamic-update-slice_fusion.7
  94.0 0.5 convolution_dynamic-update-slice_fusion.6
  94.5 0.4 convolution_dynamic-update-slice_fusion.5
  95.3 0.5 convolution_dynamic-update-slice_fusion.3
  95.7 0.4 convolution_dynamic-update-slice_fusion.2
  96.1 0.5 convolution_dynamic-update-slice_fusion.1
  96.6 0.5 convolution_dynamic-update-slice_fusion
  97.1 0.8 copy-done
  97.9 17.6 %fusion.12 = f32[64,1,56,128]{3,0,2,1:T(8,128)} fusion(f32[56,128,64]{1,2,0:T(8,128)} %fusion.16, f32[56,128,64]{1,2,0:T(8,128)} %fusion.17, f32[56,128,64]{1,2,0:T(8,128)} %fusion.18, f32[56,128,64]{1,2,0:T(8,128)} %fusion.39, f32[56,128,64]{1,2,0:T(8,128)} %fusion.19, f32[56,128,64]{1,2,0:T(8,128)} %fusion.20, f32[56,128,64]{1,2,0:T(8,128)} %fusion.21, ...), kind=kOutput, calls=%fused_computation.25 | convolution fusion | flops 41287680 | bytes 50012160 | tf_op jit(solution)/shard_map/fc,fzyx->czyx/dot_general | solution.py:39
  115.6 73.8 %all-reduce.4.cloned.1.call-done = f32[32,64,3,3,3]{1,0,4,3,2:T(8,128)} async-done(((f32[32,64,3,3,3]{1,0,4,3,2:T(8,128)}), f32[32,64,3,3,3]{1,0,4,3,2:T(8,128)}) %all-reduce.4.cloned.1.call-update) | async-done | bytes 221200 | tf_op jit(solution)/shard_map/psum | solution.py:80
  189.4 1.8 broadcast_multiply_fusion
  191.3 1.3 convert_element_type.7
  192.5 0.9 copy.9
  (16 shorter events, 1.6 us)
Async XLA Ops:
  8.0 26.8 %copy-start.1 = (bf16[32,64,3,3,3]{1,0,4,3,2:T(8,128)(2,1)S(1)}, bf16[32,64,3,3,3]{1,0,4,3,2:T(8,128)(2,1)}, u32[]{:S(2)}) copy-start(bf16[32,64,3,3,3]{1,0,4,3,2:T(8,128)(2,1)} %param.5) | copy-start | bytes 331780
  8.0 181.4 %all-reduce.4.cloned.1.call-start = ((), (), s32[]{:S(2)}) async-start(), calls=%async_computation.2 | async-start | bytes 884736 | tf_op jit(solution)/shard_map/psum | solution.py:80
  9.4 27.1 %collective-permute-start.1 = (bf16[32,1,56,128]{3,0,2,1:T(8,128)(2,1)S(1)}, bf16[32,1,56,128]{3,0,2,1:T(8,128)(2,1)S(1)}, u32[]{:S(2)}, u32[]{:S(2)}) collective-permute-start(bf16[32,1,56,128]{3,0,2,1:T(8,128)(2,1)S(1)} %compare_select_fusion), channel_id=1, source_target_pairs={{2,0},{4,2},{6,4},{8,6},{10,8},{12,10},{14,12},{16,14},{18,16},{20... | collective-permute-start | bytes 1376264 | tf_op jit(solution)/shard_map/ppermute | solution.py:15
  11.4 25.2 %collective-permute-start = (bf16[32,1,56,128]{3,0,2,1:T(8,128)(2,1)S(1)}, bf16[32,1,56,128]{3,0,2,1:T(8,128)(2,1)S(1)}, u32[]{:S(2)}, u32[]{:S(2)}) collective-permute-start(bf16[32,1,56,128]{3,0,2,1:T(8,128)(2,1)S(1)} %compare_select_fusion), channel_id=1, source_target_pairs={{0,2},{2,4},{4,6},{6,8},{8,10},{10,12},{12,14},{14,16},{16,18},{18... | collective-permute-start | bytes 1376264 | tf_op jit(solution)/shard_map/ppermute | solution.py:12
  29.2 52.2 %collective-permute-start.3 = (bf16[64,1,56,128]{3,0,2,1:T(8,128)(2,1)S(1)}, bf16[64,1,56,128]{3,0,2,1:T(8,128)(2,1)S(1)}, u32[]{:S(2)}, u32[]{:S(2)}) collective-permute-start(bf16[64,1,56,128]{3,0,2,1:T(8,128)(2,1)S(1)} %all_gather.3), channel_id=1, source_target_pairs={{2,0},{4,2},{6,4},{8,6},{10,8},{12,10},{14,12},{16,14},{18,16},{20... | collective-permute-start | bytes 2752520 | tf_op jit(solution)/shard_map/ppermute | solution.py:15
  31.3 50.2 %collective-permute-start.2 = (bf16[64,1,56,128]{3,0,2,1:T(8,128)(2,1)S(1)}, bf16[64,1,56,128]{3,0,2,1:T(8,128)(2,1)S(1)}, u32[]{:S(2)}, u32[]{:S(2)}) collective-permute-start(bf16[64,1,56,128]{3,0,2,1:T(8,128)(2,1)S(1)} %all_gather.3), channel_id=1, source_target_pairs={{0,2},{2,4},{4,6},{6,8},{8,10},{10,12},{12,14},{14,16},{16,18},{18... | collective-permute-start | bytes 2752520 | tf_op jit(solution)/shard_map/ppermute | solution.py:12
  97.1 0.8 copy-start
  97.9 93.4 %reduce-scatter.2.cloned.1.call-start = ((), (), s32[]{:S(2)}) async-start(), calls=%async_computation.1 | async-start | bytes 2752512 | tf_op jit(solution)/shard_map/reduce_scatter | solution.py:76
Sparse Core Ops, SparseCore 0:
  98.0 91.3 all-reduce.3
Sparse Core Ops, SparseCore 1:
  115.7 29.8 reduce-scatter.1
where the time goes:
time: 201 us
  matrix products  73.9 us (37%)
  waiting for transfers between devices  73.9 us (37%)
  between operations  15.7 us (8%)
  blocking collectives  12.3 us (6%)
  starting transfers between devices  12.1 us (6%)
  other arithmetic  10.3 us (5%)
  local copies, waits for them, and re-layouts  2.84 us (1%)
    psum x1, waiting for transfers between devices, on_device(): kernel_grad = lax.psum(local_terms, 'space') * scale  73.8 us
    dot_general x27, matrix products, data_grad(): jnp.einsum('fc,fzyx->czyx', weight[:, :, depth_off, row_off, col_off], pi...  62.3 us
    all_gather x1, blocking collectives, on_device(): every_chan = lax.all_gather(activations, 'filt', axis=0, tiled=True)  12.3 us
    dot_general x27, matrix products, weight_grad(): jnp.einsum('fzyx,czyx->fc', grad, piece, preferred_element_type=jnp.float32)  11.5 us
    ppermute x2, starting transfers between devices, with_halo(): lax.ppermute(lax.slice_in_dim(block, block.shape[dim] - width, None, axis...  7.99 us
    concatenate x2, other arithmetic, with_halo(): block = jnp.concatenate([low, block, high], axis=dim)  5.86 us
  transfers between devices with their start and end apart: 6, of which 1 were waited for; matrix products, arithmetic and copies ran while one was open for 33% of the time, Pallas kernels for 0%

commit v1 on v0

v1 whole, which is shorter than its diff:
```python
import functools

import jax
import jax.numpy as jnp
from jax import lax
from jax.experimental import pallas as pl
from jax.experimental.pallas import tpu as pltpu
from jax.sharding import PartitionSpec as P

MESH = pl.DeviceIdType.MESH
LANES = 128


def kernel_body(
    dims, m_ref, a_ref, k_ref, ig_ref, kg_ref,
    mbuf, abuf, kbuf, ktr, gbuf, rbuf, sbuf, obuf,
    m_recv, sp_send, fl_send, spf_send, flf_send, k_send, k_recv,
    rs_send, rs_recv, ag_send, ag_recv,
):
    S, J, fl, H, R, own, scale = dims
    s = lax.axis_index("space")
    j = lax.axis_index("filt")
    half = (H // 2) * LANES
    cells = H * LANES
    parts = (pl.ds(LANES, half), pl.ds(LANES + half, cells - half))
    k3 = 3 * J * fl

    barrier = pltpu.get_barrier_semaphore()
    count = S * J

    @pl.loop(1, count)
    def _(step):
        other = lax.rem(s * J + j + step, count)
        pl.semaphore_signal(
            barrier, inc=1, device_id={"space": other // J, "filt": lax.rem(other, J)},
            device_id_type=MESH,
        )

    edge = jnp.zeros((3, J, fl, LANES), jnp.bfloat16)
    mbuf[:, :, :, :LANES] = edge
    mbuf[:, :, :, LANES + cells :] = edge
    mbuf[1, j, :, LANES : LANES + cells] = m_ref[...]

    @pl.when(s == 0)
    def _():
        mbuf[0, :, :, LANES : LANES + cells] = jnp.zeros((J, fl, cells), jnp.bfloat16)

    @pl.when(s == S - 1)
    def _():
        mbuf[2, :, :, LANES : LANES + cells] = jnp.zeros((J, fl, cells), jnp.bfloat16)

    pl.semaphore_wait(barrier, count - 1)

    def slab_copy(slot, owner, part, to_slot, space, filt, send):
        return pltpu.make_async_remote_copy(
            src_ref=mbuf.at[slot, owner, :, parts[part]],
            dst_ref=mbuf.at[to_slot, owner, :, parts[part]],
            send_sem=send,
            recv_sem=m_recv.at[to_slot, owner, part],
            device_id={"space": space, "filt": filt},
            device_id_type=MESH,
        )

    def arrived(slot, owner, part):
        ref = mbuf.at[slot, owner, :, parts[part]]
        pltpu.make_async_copy(ref, ref, m_recv.at[slot, owner, part]).wait()

    def valid(d):
        return s > 0 if d < 0 else s < S - 1

    def far(d):
        return lax.rem(s, 2) == (0 if d < 0 else 1)

    def peer(p):
        return lax.rem(j + p, J)

    def k_copy(p):
        return pltpu.make_async_remote_copy(
            src_ref=k_ref.at[peer(p)], dst_ref=kbuf.at[j],
            send_sem=k_send.at[p - 1], recv_sem=k_recv.at[j],
            device_id={"space": s, "filt": peer(p)}, device_id_type=MESH,
        )

    def space_copy(d, part):
        return slab_copy(1, j, part, 1 - d, s + d, j, sp_send.at[(d + 1) // 2, part])

    def filt_copy(p, part):
        return slab_copy(1, j, part, 1, s, peer(p), fl_send.at[p - 1, part])

    def space_forward(d, p, part):
        return slab_copy(
            1, peer(p), part, 1 - d, s + d, j, spf_send.at[(d + 1) // 2, p - 1, part]
        )

    def filt_forward(d, p):
        return slab_copy(1 + d, j, 0, 1 + d, s, peer(p), flf_send.at[(d + 1) // 2, p - 1])

    for first in (0, 1):
        for p in range(1, J):
            filt_copy(p, 1 - first).start()
        for d in (-1, 1):
            @pl.when(valid(d))
            def _():
                space_copy(d, first).start()
    for p in range(1, J):
        k_copy(p).start()

    cl = a_ref.shape[0]
    abuf[...] = jnp.zeros_like(abuf)
    column = lax.broadcasted_iota(jnp.int32, (cl, LANES), 1)

    @pl.loop(0, H)
    def _(row):
        base = pl.multiple_of(row * LANES, LANES)
        x = a_ref[:, pl.ds(base, LANES)].astype(jnp.float32)
        left = jnp.where(column == 0, 0.0, pltpu.roll(x, 1, 1))
        right = jnp.where(column == LANES - 1, 0.0, pltpu.roll(x, LANES - 1, 1))
        to = pl.ds(pl.multiple_of(row * LANES + LANES, LANES), LANES)
        abuf[0:cl, to] = left.astype(jnp.bfloat16)
        abuf[cl : 2 * cl, to] = x.astype(jnp.bfloat16)
        abuf[2 * cl : 3 * cl, to] = right.astype(jnp.bfloat16)

    kbuf[j] = k_ref[j]

    for p in range(1, J):
        arrived(1, peer(p), 1)
        for d in (-1, 1):
            @pl.when(valid(d))
            def _():
                space_forward(d, p, 1).start()
    for d in (-1, 1):
        @pl.when(valid(d))
        def _():
            arrived(1 + d, j, 0)

            @pl.when(far(d))
            def _():
                for p in range(1, J):
                    filt_forward(d, p).start()
    for p in range(1, J):
        arrived(1, peer(p), 0)
        for d in (-1, 1):
            @pl.when(jnp.logical_and(valid(d), jnp.logical_not(far(d))))
            def _():
                space_forward(d, p, 0).start()

    def weight_terms(slot, init):
        if init:
            for q in range(J):
                for dh in range(3):
                    gbuf[q, (dh * 3 + slot) * fl : (dh * 3 + slot + 1) * fl, :] = jnp.zeros(
                        (fl, LANES), jnp.float32
                    )
        rows = 8 if H % 8 == 0 else 1

        @pl.loop(0, H // rows)
        def _(i):
            base = pl.multiple_of(i * rows * LANES, LANES)
            lhs = mbuf[slot, :, :, pl.ds(base + LANES, rows * LANES)].reshape(
                J * fl, rows * LANES
            )
            for dh in range(3):
                rhs = abuf[:, pl.ds(base + dh * LANES, rows * LANES)]
                term = lax.dot_general(
                    lhs, rhs, (((1,), (1,)), ((), ())), preferred_element_type=jnp.float32
                )
                for q in range(J):
                    to = slice((dh * 3 + slot) * fl, (dh * 3 + slot + 1) * fl)
                    gbuf[q, to, :] = gbuf[q, to, :] + term[q * fl : (q + 1) * fl]

    weight_terms(1, True)

    for p in range(1, J):
        got = kbuf.at[peer(p)]
        pltpu.make_async_copy(got, got, k_recv.at[peer(p)]).wait()
    for dh in range(3):
        stacked = jnp.concatenate(
            [kbuf[q, dh, slot] for slot in range(3) for q in range(J)], axis=0
        )
        ktr[dh] = stacked.astype(jnp.float32).T.astype(jnp.bfloat16)

    for d in (-1, 1):
        @pl.when(valid(d))
        def _():
            arrived(1 + d, j, 1)
            for p in range(1, J):
                arrived(1 + d, peer(p), 0)
                arrived(1 + d, peer(p), 1)
        weight_terms(1 + d, True)

    def rs_copy(q, t):
        return pltpu.make_async_remote_copy(
            src_ref=gbuf.at[q, pl.ds(pl.multiple_of(t * R, 8), R)],
            dst_ref=rbuf.at[s, j],
            send_sem=rs_send.at[q, t], recv_sem=rs_recv,
            device_id={"space": t, "filt": q}, device_id_type=MESH,
        )

    def rs_each(act):
        @pl.loop(0, S)
        def _(step):
            t = lax.rem(s + step, S)

            @pl.when(t < own)
            def _():
                for p in range(J):
                    q = peer(p)
                    if p > 0:
                        act(rs_copy(q, t))
                    else:
                        @pl.when(step > 0)
                        def _():
                            act(rs_copy(q, t))

    rs_each(lambda c: c.start())

    @pl.when(s < own)
    def _():
        pltpu.make_async_copy(
            gbuf.at[j, pl.ds(pl.multiple_of(s * R, 8), R)], rbuf.at[s, j], rs_recv
        ).start()

    rows = 4 if H % 4 == 0 else 1
    wide = rows * LANES
    cols = lax.rem(lax.broadcasted_iota(jnp.int32, (cl, wide), 1), LANES)

    @pl.loop(0, H // rows)
    def _(i):
        total = jnp.zeros((3 * cl, wide), jnp.float32)
        for dh in range(3):
            base = pl.multiple_of((i * rows + 2 - dh) * LANES, LANES)
            rhs = mbuf[:, :, :, pl.ds(base, wide)].reshape(k3, wide)
            total = total + jnp.dot(
                ktr[dh, : 3 * cl], rhs, preferred_element_type=jnp.float32
            )
        first = pltpu.roll(total[:cl], wide - 1, 1)
        last = pltpu.roll(total[2 * cl :], 1, 1)
        result = total[cl : 2 * cl] + jnp.where(cols == LANES - 1, 0.0, first)
        result = result + jnp.where(cols == 0, 0.0, last)
        ig_ref[:, pl.ds(pl.multiple_of(i * wide, LANES), wide)] = result.astype(jnp.bfloat16)

    def ag_copy(t):
        return pltpu.make_async_remote_copy(
            src_ref=sbuf, dst_ref=obuf.at[s], send_sem=ag_send.at[t], recv_sem=ag_recv,
            device_id={"space": t, "filt": j}, device_id_type=MESH,
        )

    def ag_each(act):
        @pl.loop(1, S)
        def _(step):
            act(ag_copy(lax.rem(s + step, S)))

    @pl.when(s < own)
    def _():
        pltpu.make_async_copy(rbuf, rbuf, rs_recv).wait()
        total = rbuf[0]
        for t in range(1, S):
            total = total + rbuf[t]
        sbuf[...] = total * scale
        ag_each(lambda c: c.start())
        pltpu.make_async_copy(sbuf, obuf.at[s], ag_recv).start()

    pltpu.make_async_copy(obuf, obuf, ag_recv).wait()
    kg_ref[...] = obuf[...]

    for first in (0, 1):
        for p in range(1, J):
            filt_copy(p, 1 - first).wait_send()
        for d in (-1, 1):
            @pl.when(valid(d))
            def _():
                space_copy(d, first).wait_send()
    for p in range(1, J):
        k_copy(p).wait_send()
        for d in (-1, 1):
            @pl.when(valid(d))
            def _():
                space_forward(d, p, 1).wait_send()

                @pl.when(far(d))
                def _():
                    filt_forward(d, p).wait_send()

                @pl.when(jnp.logical_not(far(d)))
                def _():
                    space_forward(d, p, 0).wait_send()
    rs_each(lambda c: c.wait_send())

    @pl.when(s < own)
    def _():
        ag_each(lambda c: c.wait_send())


def on_device(activations, kernel, preact, upstream):
    S, J = lax.axis_size("space"), lax.axis_size("filt")
    fl, depth, H, W = preact.shape
    cl = activations.shape[0]
    cells = H * W
    volume = S * depth * cells
    scale = 1.0 / float(volume) ** 0.5
    masked = jnp.where(preact > 0, upstream, jnp.zeros_like(upstream)).reshape(fl, cells)
    acts = activations.reshape(cl, cells)
    weights = kernel.reshape(fl, J, cl, 3, 3, 3)[:, :, :, ::-1]
    weights = weights.transpose(1, 4, 3, 0, 5, 2).reshape(J, 3, 3, fl, 3 * cl)
    weights = jnp.pad(weights, ((0, 0),) * 4 + ((0, LANES - 3 * cl),))
    tiles = 9 * fl // 8
    R = 8 * -(-tiles // S)
    own = 9 * fl // R
    dims = (S, J, fl, H, R, own, scale)
    padded = cells + 2 * W
    dma = pltpu.SemaphoreType.DMA
    vmem = pl.BlockSpec(memory_space=pltpu.VMEM)
    peers = max(J - 1, 1)
    ig, kg = pl.pallas_call(
        functools.partial(kernel_body, dims),
        out_shape=(
            jax.ShapeDtypeStruct((cl, cells), jnp.bfloat16),
            jax.ShapeDtypeStruct((own, J, R, LANES), jnp.float32),
        ),
        in_specs=[vmem] * 3,
        out_specs=(vmem, vmem),
        scratch_shapes=[
            pltpu.VMEM((3, J, fl, padded), jnp.bfloat16),
            pltpu.VMEM((LANES, padded), jnp.bfloat16),
            pltpu.VMEM((J, 3, 3, fl, LANES), jnp.bfloat16),
            pltpu.VMEM((3, LANES, 3 * J * fl), jnp.bfloat16),
            pltpu.VMEM((J, 9 * fl, LANES), jnp.float32),
            pltpu.VMEM((S, J, R, LANES), jnp.float32),
            pltpu.VMEM((J, R, LANES), jnp.float32),
            pltpu.VMEM((own, J, R, LANES), jnp.float32),
            dma((3, J, 2)), dma((2, 2)), dma((peers, 2)), dma((2, peers, 2)),
            dma((2, peers)), dma((peers,)), dma((J,)),
            dma((J, own)), dma, dma((S,)), dma,
        ],
        compiler_params=pltpu.CompilerParams(
            collective_id=0, has_side_effects=True, vmem_limit_bytes=40 * 2**20
        ),
    )(masked, acts, weights)
    input_grad = ig.reshape(cl, depth, H, W)
    kg = kg.transpose(0, 2, 1, 3).reshape(3, 3, fl, J, LANES)[:, ::-1, :, :, : 3 * cl]
    kg = kg.reshape(3, 3, fl, J, 3, cl).transpose(2, 3, 5, 1, 0, 4)
    return (input_grad, kg.reshape(fl, J * cl, 3, 3, 3))


def solution(mesh):
    in_specs = (
        P("filt", "space", None, None),
        P("filt", None, None, None, None),
        P("filt", "space", None, None),
        P("filt", "space", None, None),
    )
    out_specs = (P("filt", "space", None, None), P("filt", None, None, None, None))
    return jax.shard_map(
        on_device, mesh=mesh, in_specs=in_specs, out_specs=out_specs, check_vma=False
    )
```

time: 201 us -> 54.2 us (0.27)
  the two profiles are of different devices: /device:TPU:1 before, /device:TPU:25 now
where the time goes in v1:
time: 54.2 us; the launch traced here: 54.1 us
  Pallas kernels  47.1 us (87%)
  local copies, waits for them, and re-layouts  6.15 us (11%)
  between operations  0.74 us (1%)
    pallas_call x1, Pallas kernels, on_device(): pl.pallas_call(functools.partial(kernel_body, dims), out_shape=(jax.Shape...  47.1 us
    unnamed x7, local copies, waits for them, and re-layouts  1.57 us
    reshape x2, local copies, waits for them, and re-layouts, on_device(): weights = kernel.reshape(fl, J, cl, 3, 3, 3)[:, :, :, ::-1]  1.53 us
    reshape x1, local copies, waits for them, and re-layouts, on_device(): return (input_grad, kg.reshape(fl, J * cl, 3, 3, 3))  1.27 us

profile of v1, /device:TPU:25, one launch (start us, length us, event | category | flops | bytes accessed | tf_op | source)
XLA Modules:
  0.0 54.1 jit_solution(15880223080173705661)
XLA Ops:
  0.6 1.1 %reshape.30 = bf16[32,2,32,3,3,3]{2,1,0,5,4,3:T(2,128)(2,1)S(1)} reshape(bf16[32,64,3,3,3]{1,0,4,3,2:T(8,128)(2,1)} %param.5) | data formatting | bytes 221184 | tf_op jit(solution)/shard_map/reshape | solution.py:303
  1.8 0.4 copy.12
  2.2 0.0 copy-start.1
  2.2 0.0 copy-start.2
  2.2 0.2 reverse_bitcast_fusion
  2.4 0.0 copy-start
  2.4 0.3 reshape.31
  2.8 0.4 copy-done.1
  3.2 0.1 copy-done.2
  3.3 0.1 compare_select_fusion
  3.4 0.1 copy-done
  3.5 0.1 copy_bitcast_fusion
  3.6 47.1 %shard_map.59 = (bf16[32,7168]{1,0:T(8,128)(2,1)S(1)}, f32[12,2,24,128]{3,2,1,0:T(8,128)S(1)}) custom-call(bf16[32,7168]{1,0:T(8,128)(2,1)S(1)} %get-tuple-element.13.m_ref, bf16[32,7168]{1,0:T(8,128)(2,1)S(1)} %get-tuple-element.12.a_ref, bf16[2,3,3,32,128]{4,3,2,1,0:T(8,128)(2,1)S(1)} %pad.4.k_ref), custom_call_target="tpu_custom_call" | custom-call | tf_op jit(solution)/shard_map/pallas_call | solution.py:314
  50.7 0.8 %copy.19 = bf16[4,8,56,128]{3,2,1,0:T(8,128)(2,1)} copy(bf16[4,8,56,128]{3,1,2,0:T(8,128)(2,1)S(1)} %bitcast.30) | data formatting | bytes 917504
  51.7 0.4 reshape.34
  52.1 0.7 %copy.15 = f32[32,2,32,3,3,3]{2,1,0,5,4,3:T(2,128)S(1)} copy(f32[32,2,32,3,3,3]{2,5,0,1,3,4:T(4,128)S(1)} %bitcast.32) | data formatting | bytes 442368 | tf_op jit(solution)/shard_map/transpose | solution.py:341
  52.8 1.3 %reshape.35 = f32[32,64,3,3,3]{1,0,4,3,2:T(8,128)} reshape(f32[32,2,32,3,3,3]{2,1,0,5,4,3:T(2,128)S(1)} %copy.15) | data formatting | bytes 442368 | tf_op jit(solution)/shard_map/reshape | solution.py:342
  (4 shorter events, 0.1 us)
Async XLA Ops:
  2.2 1.0 %copy-start.1 = (bf16[32,1,56,128]{3,2,1,0:T(8,128)(2,1)S(1)}, bf16[32,1,56,128]{3,2,1,0:T(8,128)(2,1)}, u32[]{:S(2)}) copy-start(bf16[32,1,56,128]{3,2,1,0:T(8,128)(2,1)} %param.7) | copy-start | bytes 1376260
  2.2 1.1 %copy-start.2 = (bf16[32,1,56,128]{3,2,1,0:T(8,128)(2,1)S(1)}, bf16[32,1,56,128]{3,2,1,0:T(8,128)(2,1)}, u32[]{:S(2)}) copy-start(bf16[32,1,56,128]{3,2,1,0:T(8,128)(2,1)} %param.6) | copy-start | bytes 1376260
  2.4 1.1 %copy-start = (bf16[32,1,56,128]{3,2,1,0:T(8,128)(2,1)S(1)}, bf16[32,1,56,128]{3,2,1,0:T(8,128)(2,1)}, u32[]{:S(2)}) copy-start(bf16[32,1,56,128]{3,2,1,0:T(8,128)(2,1)} %param.4) | copy-start | bytes 1376260

commit v2 on v1

v2 whole, which is shorter than its diff:
```python
import functools

import jax
import jax.numpy as jnp
from jax import lax
from jax.experimental import pallas as pl
from jax.experimental.pallas import tpu as pltpu
from jax.sharding import PartitionSpec as P

MESH = pl.DeviceIdType.MESH
LANES = 128


def kernel_body(
    dims, m_ref, a_ref, k_ref, ig_ref, kg_ref,
    mbuf, abuf, kbuf, ktr, gbuf, pbuf, hbuf, rbuf, sbuf, obuf,
    m_recv, sp_send, fl_send, spf_send, flf_send, k_send, k_recv,
    pair_send, pair_recv, rs_send, rs_recv, ag_send, ag_recv, sib_send, sib_recv,
):
    S, J, fl, H, R, owners, scale = dims
    s = lax.axis_index("space")
    j = lax.axis_index("filt")
    core = lax.rem(s, 2)
    chip = s // 2
    chips = S // 2
    sibling = s + 1 - 2 * core
    keep = R * owners
    mine = (chip * owners + chips - 1) // chips
    is_owner = jnp.logical_and(mine < owners, (mine * chips) // owners == chip)
    half = (H // 2) * LANES
    cells = H * LANES
    parts = (pl.ds(LANES, half), pl.ds(LANES + half, cells - half))
    k3 = 3 * J * fl
    cl = a_ref.shape[0]

    def valid(d):
        return s > 0 if d < 0 else s < S - 1

    def far(d):
        return core == (0 if d < 0 else 1)

    def peer(p):
        return lax.rem(j + p, J)

    barrier = pltpu.get_barrier_semaphore()
    for d in (-1, 1):
        @pl.when(valid(d))
        def _():
            pl.semaphore_signal(
                barrier, inc=1, device_id={"space": s + d, "filt": j}, device_id_type=MESH
            )

    @pl.loop(1, chips * J)
    def _(step):
        other = lax.rem(chip * J + j + step, chips * J)
        pl.semaphore_signal(
            barrier, inc=1,
            device_id={"space": 2 * (other // J) + core, "filt": lax.rem(other, J)},
            device_id_type=MESH,
        )

    edge = jnp.zeros((3, J, fl, LANES), jnp.bfloat16)
    mbuf[:, :, :, :LANES] = edge
    mbuf[:, :, :, LANES + cells :] = edge
    mbuf[1, j, :, LANES : LANES + cells] = m_ref[...]

    @pl.when(s == 0)
    def _():
        mbuf[0, :, :, LANES : LANES + cells] = jnp.zeros((J, fl, cells), jnp.bfloat16)

    @pl.when(s == S - 1)
    def _():
        mbuf[2, :, :, LANES : LANES + cells] = jnp.zeros((J, fl, cells), jnp.bfloat16)

    next_to = (s > 0).astype(jnp.int32) + (s < S - 1).astype(jnp.int32)
    pl.semaphore_wait(barrier, chips * J - 1 + next_to)

    def slab_copy(slot, owner, part, to_slot, space, filt, send):
        return pltpu.make_async_remote_copy(
            src_ref=mbuf.at[slot, owner, :, parts[part]],
            dst_ref=mbuf.at[to_slot, owner, :, parts[part]],
            send_sem=send,
            recv_sem=m_recv.at[to_slot, owner, part],
            device_id={"space": space, "filt": filt},
            device_id_type=MESH,
        )

    def arrived(slot, owner, part):
        ref = mbuf.at[slot, owner, :, parts[part]]
        pltpu.make_async_copy(ref, ref, m_recv.at[slot, owner, part]).wait()

    def k_copy(p):
        return pltpu.make_async_remote_copy(
            src_ref=k_ref.at[peer(p)], dst_ref=kbuf.at[j],
            send_sem=k_send.at[p - 1], recv_sem=k_recv.at[j],
            device_id={"space": s, "filt": peer(p)}, device_id_type=MESH,
        )

    def space_copy(d, part):
        return slab_copy(1, j, part, 1 - d, s + d, j, sp_send.at[(d + 1) // 2, part])

    def filt_copy(p, part):
        return slab_copy(1, j, part, 1, s, peer(p), fl_send.at[p - 1, part])

    def space_forward(d, p, part):
        return slab_copy(
            1, peer(p), part, 1 - d, s + d, j, spf_send.at[(d + 1) // 2, p - 1, part]
        )

    def filt_forward(d, p):
        return slab_copy(1 + d, j, 0, 1 + d, s, peer(p), flf_send.at[(d + 1) // 2, p - 1])

    for first in (0, 1):
        for p in range(1, J):
            filt_copy(p, 1 - first).start()
        for d in (-1, 1):
            @pl.when(valid(d))
            def _():
                space_copy(d, first).start()
    for p in range(1, J):
        k_copy(p).start()

    abuf[...] = jnp.zeros_like(abuf)
    gbuf[...] = jnp.zeros_like(gbuf)
    kbuf[j] = k_ref[j]
    column = lax.broadcasted_iota(jnp.int32, (cl, LANES), 1)

    @pl.loop(0, H)
    def _(row):
        base = pl.multiple_of(row * LANES, LANES)
        x = a_ref[:, pl.ds(base, LANES)].astype(jnp.float32)
        left = jnp.where(column == 0, 0.0, pltpu.roll(x, 1, 1))
        right = jnp.where(column == LANES - 1, 0.0, pltpu.roll(x, LANES - 1, 1))
        to = pl.ds(pl.multiple_of(row * LANES + LANES, LANES), LANES)
        abuf[0:cl, to] = left.astype(jnp.bfloat16)
        abuf[cl : 2 * cl, to] = x.astype(jnp.bfloat16)
        abuf[2 * cl : 3 * cl, to] = right.astype(jnp.bfloat16)

    def weight_terms(pieces, part):
        rows = H // 4

        @pl.loop(2 * part, 2 * part + 2)
        def _(i):
            base = pl.multiple_of(i * rows * LANES, LANES)
            lhs = jnp.concatenate(
                [mbuf[slot, q, :, pl.ds(base + LANES, rows * LANES)] for slot, q in pieces],
                axis=0,
            )
            for dh in range(3):
                rhs = abuf[:, pl.ds(base + dh * LANES, rows * LANES)]
                term = lax.dot_general(
                    lhs, rhs, (((1,), (1,)), ((), ())), preferred_element_type=jnp.float32
                )
                for n, (slot, q) in enumerate(pieces):
                    to = slice((dh * 3 + slot) * fl, (dh * 3 + slot + 1) * fl)
                    gbuf[q, to, :] = gbuf[q, to, :] + term[n * fl : (n + 1) * fl]

    centre = [(1, q) for q in range(J)]
    own_next = [(0, j), (2, j)]
    other_next = [(slot, peer(p)) for p in range(1, J) for slot in (0, 2)]

    for p in range(1, J):
        arrived(1, peer(p), 1)
        for d in (-1, 1):
            @pl.when(valid(d))
            def _():
                space_forward(d, p, 1).start()
    for d in (-1, 1):
        @pl.when(valid(d))
        def _():
            arrived(1 + d, j, 0)

            @pl.when(far(d))
            def _():
                for p in range(1, J):
                    filt_forward(d, p).start()
    weight_terms(centre, 1)
    weight_terms(own_next, 0)
    for p in range(1, J):
        arrived(1, peer(p), 0)
        for d in (-1, 1):
            @pl.when(jnp.logical_and(valid(d), jnp.logical_not(far(d))))
            def _():
                space_forward(d, p, 0).start()
    weight_terms(centre, 0)
    for d in (-1, 1):
        @pl.when(valid(d))
        def _():
            arrived(1 + d, j, 1)
    weight_terms(own_next, 1)

    for p in range(1, J):
        got = kbuf.at[peer(p)]
        pltpu.make_async_copy(got, got, k_recv.at[peer(p)]).wait()
    for dh in range(3):
        stacked = jnp.concatenate(
            [kbuf[q, dh, slot] for slot in range(3) for q in range(J)], axis=0
        )
        ktr[dh] = stacked.astype(jnp.float32).T.astype(jnp.bfloat16)

    for part in (1, 0):
        for d in (-1, 1):
            @pl.when(valid(d))
            def _():
                for p in range(1, J):
                    arrived(1 + d, peer(p), part)
        if J > 1:
            weight_terms(other_next, part)

    def pair_copy():
        return pltpu.make_async_remote_copy(
            src_ref=gbuf.at[:, pl.ds(pl.multiple_of((1 - core) * keep, 8), keep)],
            dst_ref=pbuf, send_sem=pair_send, recv_sem=pair_recv,
            device_id={"space": sibling, "filt": j}, device_id_type=MESH,
        )

    def rs_copy(q, o):
        return pltpu.make_async_remote_copy(
            src_ref=hbuf.at[q, pl.ds(pl.multiple_of(o * R, 8), R)],
            dst_ref=rbuf.at[chip, j],
            send_sem=rs_send.at[q, o], recv_sem=rs_recv,
            device_id={"space": 2 * ((o * chips) // owners) + core, "filt": q},
            device_id_type=MESH,
        )

    def rs_each(act):
        @pl.loop(0, owners)
        def _(step):
            o = lax.rem(mine + step, owners)
            for p in range(J):
                q = peer(p)
                if p > 0:
                    act(rs_copy(q, o))
                else:
                    @pl.when((o * chips) // owners != chip)
                    def _():
                        act(rs_copy(q, o))

    def ag_copy(t):
        return pltpu.make_async_remote_copy(
            src_ref=sbuf, dst_ref=obuf.at[core, mine], send_sem=ag_send.at[t],
            recv_sem=ag_recv,
            device_id={"space": 2 * t + core, "filt": j}, device_id_type=MESH,
        )

    def ag_each(act):
        @pl.loop(1, chips)
        def _(step):
            act(ag_copy(lax.rem(chip + step, chips)))

    def sib_copy():
        return pltpu.make_async_remote_copy(
            src_ref=obuf.at[core], dst_ref=obuf.at[core],
            send_sem=sib_send, recv_sem=sib_recv,
            device_id={"space": sibling, "filt": j}, device_id_type=MESH,
        )

    rows = H // 8
    wide = rows * LANES
    cols = lax.rem(lax.broadcasted_iota(jnp.int32, (cl, wide), 1), LANES)

    def input_part(first_step, last_step):
        @pl.loop(first_step, last_step)
        def _(i):
            for sub in range(2):
                at = (2 * i + sub) * rows
                total = jnp.zeros((3 * cl, wide), jnp.float32)
                for dh in range(3):
                    base = pl.multiple_of((at + 2 - dh) * LANES, LANES)
                    rhs = mbuf[:, :, :, pl.ds(base, wide)].reshape(k3, wide)
                    total = total + jnp.dot(
                        ktr[dh, : 3 * cl], rhs, preferred_element_type=jnp.float32
                    )
                first = pltpu.roll(total[:cl], wide - 1, 1)
                last = pltpu.roll(total[2 * cl :], 1, 1)
                result = total[cl : 2 * cl] + jnp.where(cols == LANES - 1, 0.0, first)
                result = result + jnp.where(cols == 0, 0.0, last)
                to = pl.ds(pl.multiple_of(at * LANES, LANES), wide)
                ig_ref[:, to] = result.astype(jnp.bfloat16)

    pair_copy().start()
    input_part(0, 1)
    pair_copy().wait_recv()
    hbuf[...] = gbuf[:, pl.ds(pl.multiple_of(core * keep, 8), keep)] + pbuf[...]
    rs_each(lambda c: c.start())

    @pl.when(is_owner)
    def _():
        pltpu.make_async_copy(
            hbuf.at[j, pl.ds(pl.multiple_of(mine * R, 8), R)], rbuf.at[chip, j], rs_recv
        ).start()

    input_part(1, 3)

    @pl.when(is_owner)
    def _():
        pltpu.make_async_copy(rbuf, rbuf, rs_recv).wait()
        total = rbuf[0]
        for t in range(1, chips):
            total = total + rbuf[t]
        sbuf[...] = total * scale
        ag_each(lambda c: c.start())
        pltpu.make_async_copy(sbuf, obuf.at[core, mine], ag_recv).start()

    input_part(3, 4)
    pltpu.make_async_copy(obuf.at[core], obuf.at[core], ag_recv).wait()
    sib_copy().start()
    kg_ref[core] = obuf[core]
    sib_copy().wait_recv()
    kg_ref[1 - core] = obuf[1 - core]

    for first in (0, 1):
        for p in range(1, J):
            filt_copy(p, 1 - first).wait_send()
        for d in (-1, 1):
            @pl.when(valid(d))
            def _():
                space_copy(d, first).wait_send()
    for p in range(1, J):
        k_copy(p).wait_send()
        for d in (-1, 1):
            @pl.when(valid(d))
            def _():
                space_forward(d, p, 1).wait_send()

                @pl.when(far(d))
                def _():
                    filt_forward(d, p).wait_send()

                @pl.when(jnp.logical_not(far(d)))
                def _():
                    space_forward(d, p, 0).wait_send()
    pair_copy().wait_send()
    rs_each(lambda c: c.wait_send())

    @pl.when(is_owner)
    def _():
        ag_each(lambda c: c.wait_send())

    sib_copy().wait_send()


def on_device(activations, kernel, preact, upstream):
    S, J = lax.axis_size("space"), lax.axis_size("filt")
    fl, depth, H, W = preact.shape
    cl = activations.shape[0]
    cells = H * W
    volume = S * depth * cells
    scale = 1.0 / float(volume) ** 0.5
    masked = jnp.where(preact > 0, upstream, jnp.zeros_like(upstream)).reshape(fl, cells)
    acts = activations.reshape(cl, cells)
    weights = kernel.reshape(fl, J, cl, 3, 3, 3)[:, :, :, ::-1]
    weights = weights.transpose(1, 4, 3, 0, 5, 2).reshape(J, 3, 3, fl, 3 * cl)
    weights = jnp.pad(weights, ((0, 0),) * 4 + ((0, LANES - 3 * cl),))
    chips = S // 2
    tiles = -(-9 * fl // 16)
    R = 8 * -(-tiles // chips)
    owners = -(-8 * tiles // R)
    keep = R * owners
    dims = (S, J, fl, H, R, owners, scale)
    padded = cells + 2 * W
    dma = pltpu.SemaphoreType.DMA
    vmem = pl.BlockSpec(memory_space=pltpu.VMEM)
    peers = max(J - 1, 1)
    ig, kg = pl.pallas_call(
        functools.partial(kernel_body, dims),
        out_shape=(
            jax.ShapeDtypeStruct((cl, cells), jnp.bfloat16),
            jax.ShapeDtypeStruct((2, owners, J, R, LANES), jnp.float32),
        ),
        in_specs=[vmem] * 3,
        out_specs=(vmem, vmem),
        scratch_shapes=[
            pltpu.VMEM((3, J, fl, padded), jnp.bfloat16),
            pltpu.VMEM((LANES, padded), jnp.bfloat16),
            pltpu.VMEM((J, 3, 3, fl, LANES), jnp.bfloat16),
            pltpu.VMEM((3, LANES, 3 * J * fl), jnp.bfloat16),
            pltpu.VMEM((J, 2 * keep, LANES), jnp.float32),
            pltpu.VMEM((J, keep, LANES), jnp.float32),
            pltpu.VMEM((J, keep, LANES), jnp.float32),
            pltpu.VMEM((chips, J, R, LANES), jnp.float32),
            pltpu.VMEM((J, R, LANES), jnp.float32),
            pltpu.VMEM((2, owners, J, R, LANES), jnp.float32),
            dma((3, J, 2)), dma((2, 2)), dma((peers, 2)), dma((2, peers, 2)),
            dma((2, peers)), dma((peers,)), dma((J,)),
            dma, dma, dma((J, owners)), dma, dma((chips,)), dma, dma, dma,
        ],
        compiler_params=pltpu.CompilerParams(
            collective_id=0, has_side_effects=True, vmem_limit_bytes=40 * 2**20
        ),
    )(masked, acts, weights)
    input_grad = ig.reshape(cl, depth, H, W)
    kg = kg.transpose(0, 1, 3, 2, 4).reshape(2 * keep, J, LANES)[: 9 * fl]
    kg = kg.reshape(3, 3, fl, J, LANES)[:, ::-1, :, :, : 3 * cl]
    kg = kg.reshape(3, 3, fl, J, 3, cl).transpose(2, 3, 5, 1, 0, 4)
    return (input_grad, kg.reshape(fl, J * cl, 3, 3, 3))


def solution(mesh):
    in_specs = (
        P("filt", "space", None, None),
        P("filt", None, None, None, None),
        P("filt", "space", None, None),
        P("filt", "space", None, None),
    )
    out_specs = (P("filt", "space", None, None), P("filt", None, None, None, None))
    return jax.shard_map(
        on_device, mesh=mesh, in_specs=in_specs, out_specs=out_specs, check_vma=False
    )
```

time: 54.2 us -> 45.5 us (0.84)
  the two profiles are of different devices: /device:TPU:25 before, /device:TPU:1 now
where the time goes in v2:
time: 45.5 us; the launch traced here: 45.3 us
  Pallas kernels  38.4 us (84%)
  local copies, waits for them, and re-layouts  6.15 us (14%)
  between operations  0.74 us (2%)
    pallas_call x1, Pallas kernels, on_device(): pl.pallas_call(functools.partial(kernel_body, dims), out_shape=(jax.Shape...  38.4 us
    unnamed x7, local copies, waits for them, and re-layouts  1.57 us
    reshape x2, local copies, waits for them, and re-layouts, on_device(): weights = kernel.reshape(fl, J, cl, 3, 3, 3)[:, :, :, ::-1]  1.53 us
    reshape x1, local copies, waits for them, and re-layouts, on_device(): return (input_grad, kg.reshape(fl, J * cl, 3, 3, 3))  1.27 us

profile of v2, /device:TPU:1, one launch (start us, length us, event | category | flops | bytes accessed | tf_op | source)
XLA Modules:
  0.0 45.3 jit_solution(4840655821078923308)
XLA Ops:
  0.6 1.1 %reshape.27 = bf16[32,2,32,3,3,3]{2,1,0,5,4,3:T(2,128)(2,1)S(1)} reshape(bf16[32,64,3,3,3]{1,0,4,3,2:T(8,128)(2,1)} %param.5) | data formatting | bytes 221184 | tf_op jit(solution)/shard_map/reshape | solution.py:352
  1.8 0.4 copy.12
  2.2 0.0 copy-start.1
  2.2 0.0 copy-start.2
  2.2 0.2 reverse_bitcast_fusion
  2.4 0.0 copy-start
  2.4 0.3 reshape.28
  2.8 0.4 copy-done.1
  3.2 0.1 copy-done.2
  3.3 0.1 compare_select_fusion
  3.4 0.1 copy-done
  3.5 0.1 copy_bitcast_fusion
  3.6 38.4 %shard_map.59 = (bf16[32,7168]{1,0:T(8,128)(2,1)S(1)}, f32[2,6,2,24,128]{4,3,2,1,0:T(8,128)S(1)}) custom-call(bf16[32,7168]{1,0:T(8,128)(2,1)S(1)} %get-tuple-element.13.m_ref, bf16[32,7168]{1,0:T(8,128)(2,1)S(1)} %get-tuple-element.12.a_ref, bf16[2,3,3,32,128]{4,3,2,1,0:T(8,128)(2,1)S(1)} %pad.4.k_ref), custom_call_target="tpu_custom_call" | custom-call | tf_op jit(solution)/shard_map/pallas_call | solution.py:365
  42.0 0.8 %copy.19 = bf16[4,8,56,128]{3,2,1,0:T(8,128)(2,1)} copy(bf16[4,8,56,128]{3,1,2,0:T(8,128)(2,1)S(1)} %bitcast.30) | data formatting | bytes 917504
  42.9 0.4 reshape.30
  43.4 0.7 %copy.15 = f32[32,2,32,3,3,3]{2,1,0,5,4,3:T(2,128)S(1)} copy(f32[32,2,32,3,3,3]{2,5,0,1,3,4:T(4,128)S(1)} %bitcast.32) | data formatting | bytes 442368 | tf_op jit(solution)/shard_map/transpose | solution.py:395
  44.1 1.3 %reshape.31 = f32[32,64,3,3,3]{1,0,4,3,2:T(8,128)} reshape(f32[32,2,32,3,3,3]{2,1,0,5,4,3:T(2,128)S(1)} %copy.15) | data formatting | bytes 442368 | tf_op jit(solution)/shard_map/reshape | solution.py:396
  (4 shorter events, 0.1 us)
Async XLA Ops:
  2.2 1.0 %copy-start.1 = (bf16[32,1,56,128]{3,2,1,0:T(8,128)(2,1)S(1)}, bf16[32,1,56,128]{3,2,1,0:T(8,128)(2,1)}, u32[]{:S(2)}) copy-start(bf16[32,1,56,128]{3,2,1,0:T(8,128)(2,1)} %param.7) | copy-start | bytes 1376260
  2.2 1.1 %copy-start.2 = (bf16[32,1,56,128]{3,2,1,0:T(8,128)(2,1)S(1)}, bf16[32,1,56,128]{3,2,1,0:T(8,128)(2,1)}, u32[]{:S(2)}) copy-start(bf16[32,1,56,128]{3,2,1,0:T(8,128)(2,1)} %param.6) | copy-start | bytes 1376260
  2.4 1.1 %copy-start = (bf16[32,1,56,128]{3,2,1,0:T(8,128)(2,1)S(1)}, bf16[32,1,56,128]{3,2,1,0:T(8,128)(2,1)}, u32[]{:S(2)}) copy-start(bf16[32,1,56,128]{3,2,1,0:T(8,128)(2,1)} %param.4) | copy-start | bytes 1376260

commit v3 on v2

--- a/solution.py
+++ b/solution.py
@@ -13,7 +13,7 @@
 
 def kernel_body(
     dims, m_ref, a_ref, k_ref, ig_ref, kg_ref,
-    mbuf, abuf, kbuf, ktr, gbuf, pbuf, hbuf, rbuf, sbuf, obuf,
+    mbuf, abuf, kpart, kbuf, ktr, gbuf, pbuf, hbuf, rbuf, sbuf, obuf,
     m_recv, sp_send, fl_send, spf_send, flf_send, k_send, k_recv,
     pair_send, pair_recv, rs_send, rs_recv, ag_send, ag_recv, sib_send, sib_recv,
 ):
@@ -91,7 +91,7 @@
 
     def k_copy(p):
         return pltpu.make_async_remote_copy(
-            src_ref=k_ref.at[peer(p)], dst_ref=kbuf.at[j],
+            src_ref=kpart.at[peer(p)], dst_ref=kbuf.at[j],
             send_sem=k_send.at[p - 1], recv_sem=k_recv.at[j],
             device_id={"space": s, "filt": peer(p)}, device_id_type=MESH,
         )
@@ -117,12 +117,10 @@
             @pl.when(valid(d))
             def _():
                 space_copy(d, first).start()
-    for p in range(1, J):
-        k_copy(p).start()
-
-    abuf[...] = jnp.zeros_like(abuf)
+
+    abuf[:LANES] = jnp.zeros((LANES, LANES), jnp.bfloat16)
+    abuf[LANES + cells :] = jnp.zeros((LANES, LANES), jnp.bfloat16)
     gbuf[...] = jnp.zeros_like(gbuf)
-    kbuf[j] = k_ref[j]
     column = lax.broadcasted_iota(jnp.int32, (cl, LANES), 1)
 
     @pl.loop(0, H)
@@ -131,10 +129,25 @@
         x = a_ref[:, pl.ds(base, LANES)].astype(jnp.float32)
         left = jnp.where(column == 0, 0.0, pltpu.roll(x, 1, 1))
         right = jnp.where(column == LANES - 1, 0.0, pltpu.roll(x, LANES - 1, 1))
+        rest = jnp.zeros((LANES - 3 * cl, LANES), jnp.float32)
+        stacked = jnp.concatenate([left, x, right, rest], axis=0)
         to = pl.ds(pl.multiple_of(row * LANES + LANES, LANES), LANES)
-        abuf[0:cl, to] = left.astype(jnp.bfloat16)
-        abuf[cl : 2 * cl, to] = x.astype(jnp.bfloat16)
-        abuf[2 * cl : 3 * cl, to] = right.astype(jnp.bfloat16)
+        abuf[to, :] = stacked.T.astype(jnp.bfloat16)
+
+    for q in range(J):
+        for dh in range(3):
+            for slot in range(3):
+                taps = [
+                    k_ref[(2 - slot) * 9 + dh * 3 + dw].astype(jnp.float32)[
+                        :, q * cl : (q + 1) * cl
+                    ]
+                    for dw in range(3)
+                ]
+                taps.append(jnp.zeros((fl, LANES - 3 * cl), jnp.float32))
+                kpart[q, dh, slot] = jnp.concatenate(taps, axis=1).astype(jnp.bfloat16)
+    for p in range(1, J):
+        k_copy(p).start()
+    kbuf[j] = kpart[j]
 
     def weight_terms(pieces, part):
         rows = H // 4
@@ -146,14 +159,16 @@
                 [mbuf[slot, q, :, pl.ds(base + LANES, rows * LANES)] for slot, q in pieces],
                 axis=0,
             )
+            rhs = jnp.concatenate(
+                [abuf[pl.ds(base + dh * LANES, rows * LANES), :] for dh in range(3)], axis=1
+            )
+            term = jnp.dot(lhs, rhs, preferred_element_type=jnp.float32)
             for dh in range(3):
-                rhs = abuf[:, pl.ds(base + dh * LANES, rows * LANES)]
-                term = lax.dot_general(
-                    lhs, rhs, (((1,), (1,)), ((), ())), preferred_element_type=jnp.float32
-                )
                 for n, (slot, q) in enumerate(pieces):
                     to = slice((dh * 3 + slot) * fl, (dh * 3 + slot + 1) * fl)
-                    gbuf[q, to, :] = gbuf[q, to, :] + term[n * fl : (n + 1) * fl]
+                    gbuf[q, to, :] = gbuf[q, to, :] + term[
+                        n * fl : (n + 1) * fl, dh * LANES : (dh + 1) * LANES
+                    ]
 
     centre = [(1, q) for q in range(J)]
     own_next = [(0, j), (2, j)]
@@ -305,9 +320,15 @@
     input_part(3, 4)
     pltpu.make_async_copy(obuf.at[core], obuf.at[core], ag_recv).wait()
     sib_copy().start()
-    kg_ref[core] = obuf[core]
     sib_copy().wait_recv()
-    kg_ref[1 - core] = obuf[1 - core]
+    blocks = [obuf[:, :, q].reshape(2 * keep, LANES) for q in range(J)]
+    for dh in range(3):
+        for slot in range(3):
+            at = (dh * 3 + slot) * fl
+            for dw in range(3):
+                kg_ref[(2 - slot) * 9 + dh * 3 + dw] = jnp.concatenate(
+                    [b[at : at + fl, dw * cl : (dw + 1) * cl] for b in blocks], axis=1
+                )
 
     for first in (0, 1):
         for p in range(1, J):
@@ -349,9 +370,7 @@
     scale = 1.0 / float(volume) ** 0.5
     masked = jnp.where(preact > 0, upstream, jnp.zeros_like(upstream)).reshape(fl, cells)
     acts = activations.reshape(cl, cells)
-    weights = kernel.reshape(fl, J, cl, 3, 3, 3)[:, :, :, ::-1]
-    weights = weights.transpose(1, 4, 3, 0, 5, 2).reshape(J, 3, 3, fl, 3 * cl)
-    weights = jnp.pad(weights, ((0, 0),) * 4 + ((0, LANES - 3 * cl),))
+    taps = kernel.transpose(2, 3, 4, 0, 1).reshape(27, fl, J * cl)
     chips = S // 2
     tiles = -(-9 * fl // 16)
     R = 8 * -(-tiles // chips)
@@ -366,13 +385,14 @@
         functools.partial(kernel_body, dims),
         out_shape=(
             jax.ShapeDtypeStruct((cl, cells), jnp.bfloat16),
-            jax.ShapeDtypeStruct((2, owners, J, R, LANES), jnp.float32),
+            jax.ShapeDtypeStruct((27, fl, J * cl), jnp.float32),
         ),
         in_specs=[vmem] * 3,
         out_specs=(vmem, vmem),
         scratch_shapes=[
             pltpu.VMEM((3, J, fl, padded), jnp.bfloat16),
-            pltpu.VMEM((LANES, padded), jnp.bfloat16),
+            pltpu.VMEM((padded, LANES), jnp.bfloat16),
+            pltpu.VMEM((J, 3, 3, fl, LANES), jnp.bfloat16),
             pltpu.VMEM((J, 3, 3, fl, LANES), jnp.bfloat16),
             pltpu.VMEM((3, LANES, 3 * J * fl), jnp.bfloat16),
             pltpu.VMEM((J, 2 * keep, LANES), jnp.float32),
@@ -388,12 +408,10 @@
         compiler_params=pltpu.CompilerParams(
             collective_id=0, has_side_effects=True, vmem_limit_bytes=40 * 2**20
         ),
-    )(masked, acts, weights)
+    )(masked, acts, taps)
     input_grad = ig.reshape(cl, depth, H, W)
-    kg = kg.transpose(0, 1, 3, 2, 4).reshape(2 * keep, J, LANES)[: 9 * fl]
-    kg = kg.reshape(3, 3, fl, J, LANES)[:, ::-1, :, :, : 3 * cl]
-    kg = kg.reshape(3, 3, fl, J, 3, cl).transpose(2, 3, 5, 1, 0, 4)
-    return (input_grad, kg.reshape(fl, J * cl, 3, 3, 3))
+    kernel_grad = kg.reshape(3, 3, 3, fl, J * cl).transpose(3, 4, 0, 1, 2)
+    return (input_grad, kernel_grad)
 
 
 def solution(mesh):

time: 45.5 us -> 42.5 us (0.934)
  local copies, waits for them, and re-layouts: 6.15 us -> 2.54 us
  other arithmetic: 0.05 us -> 1.26 us
  Pallas kernels: 38.4 us -> 37.9 us
    reshape x5 -> x0, local copies, waits for them, and re-layouts: 3.48 us -> none  [the longest x2 1.53 us: on_device(): weights = kernel.reshape(fl, J, cl, 3, 3, 3)[:, :, :, ::-1]]
    select_n x1, other arithmetic: 0.05 us -> 1.26 us  [on_device(): jnp.where(preact > 0, upstream, jnp.zeros_like(upstream)).reshape(fl, cells)]
    transpose x3 -> x0, local copies, waits for them, and re-layouts: 0.94 us -> none  [the longest x1 0.69 us: on_device(): kg = kg.reshape(3, 3, fl, J, 3, cl).transpose(2, 3, 5, 1, 0, 4)]
    unnamed x7 -> x6, local copies, waits for them, and re-layouts: 1.57 us -> 2.45 us
    pallas_call x1, Pallas kernels: 38.4 us -> 37.9 us  [on_device(): pl.pallas_call(functools.partial(kernel_body, dims), out_shape=(jax.Shape...]
where the time goes in v3:
time: 42.5 us; the launch traced here: 42.4 us
  Pallas kernels  37.9 us (89%)
  local copies, waits for them, and re-layouts  2.54 us (6%)
  other arithmetic  1.26 us (3%)
  between operations  0.66 us (2%)
    pallas_call x1, Pallas kernels, on_device(): pl.pallas_call(functools.partial(kernel_body, dims), out_shape=(jax.Shape...  37.9 us
    unnamed x6, local copies, waits for them, and re-layouts  2.45 us
    select_n x1, other arithmetic, on_device(): jnp.where(preact > 0, upstream, jnp.zeros_like(upstream)).reshape(fl, cells)  1.26 us

profile of v3, /device:TPU:1, one launch (start us, length us, event | category | flops | bytes accessed | tf_op | source)
XLA Modules:
  0.0 42.4 jit_solution(7778999558214139994)
XLA Ops:
  0.6 0.0 copy-start.1
  0.6 1.3 %compare_select_fusion = bf16[32,1,56,128]{3,2,1,0:T(8,128)(2,1)S(1)} fusion(bf16[32,1,56,128]{3,2,1,0:T(8,128)(2,1)} %param.7, bf16[32,1,56,128]{3,2,1,0:T(8,128)(2,1)} %param.6), kind=kLoop, calls=%fused_computation | loop fusion | flops 458752 | bytes 1376256 | tf_op jit(solution)/shard_map/jit(_where)/select_n | solution.py:371
  1.9 0.0 copy-done.1
  1.9 0.0 copy-start
  1.9 0.1 copy_bitcast_fusion
  2.0 0.8 %copy-done = bf16[32,64,3,3,3]{1,0,4,3,2:T(8,128)(2,1)S(1)} copy-done((bf16[32,64,3,3,3]{1,0,4,3,2:T(8,128)(2,1)S(1)}, bf16[32,64,3,3,3]{1,0,4,3,2:T(8,128)(2,1)}, u32[]{:S(2)}) %copy-start) | copy-done | bytes 110616
  2.9 37.9 %shard_map.59 = (bf16[32,7168]{1,0:T(8,128)(2,1)S(1)}, f32[27,32,64]{2,1,0:T(8,128)S(1)}) custom-call(bf16[32,7168]{1,0:T(8,128)(2,1)S(1)} %get-tuple-element.9.m_ref, bf16[32,7168]{1,0:T(8,128)(2,1)S(1)} %get-tuple-element.8.a_ref, bf16[27,32,64]{2,1,0:T(8,128)(2,1)S(1)} %bitcast.22), custom_call_target="tpu_custom_call" | custom-call | tf_op jit(solution)/shard_map/pallas_call | solution.py:384
  40.8 0.8 %copy.9 = bf16[4,8,56,128]{3,2,1,0:T(8,128)(2,1)} copy(bf16[4,8,56,128]{3,1,2,0:T(8,128)(2,1)S(1)} %bitcast.20) | data formatting | bytes 917504
  41.6 0.8 %copy.13 = f32[32,64,3,3,3]{1,0,4,3,2:T(8,128)} copy(f32[32,64,3,3,3]{1,0,4,3,2:T(8,128)S(1)} %bitcast.21) | data formatting | bytes 442368
Async XLA Ops:
  0.6 1.3 %copy-start.1 = (bf16[32,1,56,128]{3,2,1,0:T(8,128)(2,1)S(1)}, bf16[32,1,56,128]{3,2,1,0:T(8,128)(2,1)}, u32[]{:S(2)}) copy-start(bf16[32,1,56,128]{3,2,1,0:T(8,128)(2,1)} %param.4) | copy-start | bytes 1376260
  1.9 0.9 %copy-start = (bf16[32,64,3,3,3]{1,0,4,3,2:T(8,128)(2,1)S(1)}, bf16[32,64,3,3,3]{1,0,4,3,2:T(8,128)(2,1)}, u32[]{:S(2)}) copy-start(bf16[32,64,3,3,3]{1,0,4,3,2:T(8,128)(2,1)} %param.5) | copy-start | bytes 331780

commit v4 on v3

--- a/solution.py
+++ b/solution.py
@@ -170,9 +170,96 @@
                         n * fl : (n + 1) * fl, dh * LANES : (dh + 1) * LANES
                     ]
 
-    centre = [(1, q) for q in range(J)]
-    own_next = [(0, j), (2, j)]
-    other_next = [(slot, peer(p)) for p in range(1, J) for slot in (0, 2)]
+    def pair_copy(p):
+        rows_out = pl.ds(pl.multiple_of((1 - core) * keep, 8), keep)
+        return pltpu.make_async_remote_copy(
+            src_ref=gbuf.at[peer(p), rows_out], dst_ref=pbuf.at[p],
+            send_sem=pair_send.at[p], recv_sem=pair_recv.at[p],
+            device_id={"space": sibling, "filt": j}, device_id_type=MESH,
+        )
+
+    def rs_copy(p, o):
+        return pltpu.make_async_remote_copy(
+            src_ref=hbuf.at[p, pl.ds(pl.multiple_of(o * R, 8), R)],
+            dst_ref=rbuf.at[j, chip],
+            send_sem=rs_send.at[p, o], recv_sem=rs_recv.at[j],
+            device_id={"space": 2 * ((o * chips) // owners) + core, "filt": peer(p)},
+            device_id_type=MESH,
+        )
+
+    def rs_each(p, act):
+        @pl.loop(0, owners)
+        def _(step):
+            o = lax.rem(mine + step, owners)
+            if p > 0:
+                act(rs_copy(p, o))
+            else:
+                @pl.when((o * chips) // owners != chip)
+                def _():
+                    act(rs_copy(p, o))
+
+    def ag_copy(p, t):
+        return pltpu.make_async_remote_copy(
+            src_ref=sbuf.at[p], dst_ref=obuf.at[peer(p), core, mine],
+            send_sem=ag_send.at[p, t], recv_sem=ag_recv.at[peer(p)],
+            device_id={"space": 2 * t + core, "filt": j}, device_id_type=MESH,
+        )
+
+    def ag_each(p, act):
+        @pl.loop(1, chips)
+        def _(step):
+            act(ag_copy(p, lax.rem(chip + step, chips)))
+
+    def sib_copy(p):
+        ref = obuf.at[peer(p), core]
+        return pltpu.make_async_remote_copy(
+            src_ref=ref, dst_ref=ref,
+            send_sem=sib_send.at[p], recv_sem=sib_recv.at[peer(p)],
+            device_id={"space": sibling, "filt": j}, device_id_type=MESH,
+        )
+
+    def pair_start(stage):
+        for p in stage:
+            pair_copy(p).start()
+
+    def reduce_start(stage):
+        for p in stage:
+            pair_copy(p).wait_recv()
+            own_rows = pl.ds(pl.multiple_of(core * keep, 8), keep)
+            hbuf[p] = gbuf[peer(p), own_rows] + pbuf[p]
+            rs_each(p, lambda c: c.start())
+            if p == 0:
+                @pl.when(is_owner)
+                def _():
+                    pltpu.make_async_copy(
+                        hbuf.at[0, pl.ds(pl.multiple_of(mine * R, 8), R)],
+                        rbuf.at[j, chip], rs_recv.at[j],
+                    ).start()
+
+    def gather_start(stage):
+        @pl.when(is_owner)
+        def _():
+            for p in stage:
+                got = rbuf.at[peer(p)]
+                pltpu.make_async_copy(got, got, rs_recv.at[peer(p)]).wait()
+                total = rbuf[peer(p), 0]
+                for t in range(1, chips):
+                    total = total + rbuf[peer(p), t]
+                sbuf[p] = total * scale
+                ag_each(p, lambda c: c.start())
+                pltpu.make_async_copy(
+                    sbuf.at[p], obuf.at[peer(p), core, mine], ag_recv.at[peer(p)]
+                ).start()
+
+    def share_start(stage):
+        for p in stage:
+            got = obuf.at[peer(p), core]
+            pltpu.make_async_copy(got, got, ag_recv.at[peer(p)]).wait()
+            sib_copy(p).start()
+
+    early, late = range(0, 1), range(1, J)
+    own_all = [(slot, j) for slot in range(3)]
+    other_all = [(slot, peer(p)) for p in late for slot in range(3)]
 
     for p in range(1, J):
         arrived(1, peer(p), 1)
@@ -189,29 +276,28 @@
             def _():
                 for p in range(1, J):
                     filt_forward(d, p).start()
-    weight_terms(centre, 1)
-    weight_terms(own_next, 0)
+    weight_terms(own_all, 0)
     for p in range(1, J):
         arrived(1, peer(p), 0)
         for d in (-1, 1):
             @pl.when(jnp.logical_and(valid(d), jnp.logical_not(far(d))))
             def _():
                 space_forward(d, p, 0).start()
-    weight_terms(centre, 0)
     for d in (-1, 1):
         @pl.when(valid(d))
         def _():
             arrived(1 + d, j, 1)
-    weight_terms(own_next, 1)
+    weight_terms(own_all, 1)
+    pair_start(early)
 
     for p in range(1, J):
         got = kbuf.at[peer(p)]
         pltpu.make_async_copy(got, got, k_recv.at[peer(p)]).wait()
-    for dh in range(3):
-        stacked = jnp.concatenate(
-            [kbuf[q, dh, slot] for slot in range(3) for q in range(J)], axis=0
-        )
-        ktr[dh] = stacked.astype(jnp.float32).T.astype(jnp.bfloat16)
+    stacked = jnp.concatenate(
+        [kbuf[q, dh, slot] for dh in range(3) for slot in range(3) for q in range(J)], axis=0
+    )
+    ktr[...] = stacked.astype(jnp.float32).T.astype(jnp.bfloat16)
+    reduce_start(early)
 
     for part in (1, 0):
         for d in (-1, 1):
@@ -220,55 +306,10 @@
                 for p in range(1, J):
                     arrived(1 + d, peer(p), part)
         if J > 1:
-            weight_terms(other_next, part)
-
-    def pair_copy():
-        return pltpu.make_async_remote_copy(
-            src_ref=gbuf.at[:, pl.ds(pl.multiple_of((1 - core) * keep, 8), keep)],
-            dst_ref=pbuf, send_sem=pair_send, recv_sem=pair_recv,
-            device_id={"space": sibling, "filt": j}, device_id_type=MESH,
-        )
-
-    def rs_copy(q, o):
-        return pltpu.make_async_remote_copy(
-            src_ref=hbuf.at[q, pl.ds(pl.multiple_of(o * R, 8), R)],
-            dst_ref=rbuf.at[chip, j],
-            send_sem=rs_send.at[q, o], recv_sem=rs_recv,
-            device_id={"space": 2 * ((o * chips) // owners) + core, "filt": q},
-            device_id_type=MESH,
-        )
-
-    def rs_each(act):
-        @pl.loop(0, owners)
-        def _(step):
-            o = lax.rem(mine + step, owners)
-            for p in range(J):
-                q = peer(p)
-                if p > 0:
-                    act(rs_copy(q, o))
-                else:
-                    @pl.when((o * chips) // owners != chip)
-                    def _():
-                        act(rs_copy(q, o))
-
-    def ag_copy(t):
-        return pltpu.make_async_remote_copy(
-            src_ref=sbuf, dst_ref=obuf.at[core, mine], send_sem=ag_send.at[t],
-            recv_sem=ag_recv,
-            device_id={"space": 2 * t + core, "filt": j}, device_id_type=MESH,
-        )
-
-    def ag_each(act):
-        @pl.loop(1, chips)
-        def _(step):
-            act(ag_copy(lax.rem(chip + step, chips)))
-
-    def sib_copy():
-        return pltpu.make_async_remote_copy(
-            src_ref=obuf.at[core], dst_ref=obuf.at[core],
-            send_sem=sib_send, recv_sem=sib_recv,
-            device_id={"space": sibling, "filt": j}, device_id_type=MESH,
-        )
+            weight_terms(other_all, part)
+        if part == 1:
+            gather_start(early)
+    pair_start(late)
 
     rows = H // 8
     wide = rows * LANES
@@ -279,13 +320,16 @@
         def _(i):
             for sub in range(2):
                 at = (2 * i + sub) * rows
-                total = jnp.zeros((3 * cl, wide), jnp.float32)
-                for dh in range(3):
-                    base = pl.multiple_of((at + 2 - dh) * LANES, LANES)
-                    rhs = mbuf[:, :, :, pl.ds(base, wide)].reshape(k3, wide)
-                    total = total + jnp.dot(
-                        ktr[dh, : 3 * cl], rhs, preferred_element_type=jnp.float32
-                    )
+                slabs = [
+                    mbuf[
+                        :, :, :, pl.ds(pl.multiple_of((at + 2 - dh) * LANES, LANES), wide)
+                    ].reshape(k3, wide)
+                    for dh in range(3)
+                ]
+                total = jnp.dot(
+                    ktr[: 3 * cl], jnp.concatenate(slabs, axis=0),
+                    preferred_element_type=jnp.float32,
+                )
                 first = pltpu.roll(total[:cl], wide - 1, 1)
                 last = pltpu.roll(total[2 * cl :], 1, 1)
                 result = total[cl : 2 * cl] + jnp.where(cols == LANES - 1, 0.0, first)
@@ -293,35 +337,17 @@
                 to = pl.ds(pl.multiple_of(at * LANES, LANES), wide)
                 ig_ref[:, to] = result.astype(jnp.bfloat16)
 
-    pair_copy().start()
     input_part(0, 1)
-    pair_copy().wait_recv()
-    hbuf[...] = gbuf[:, pl.ds(pl.multiple_of(core * keep, 8), keep)] + pbuf[...]
-    rs_each(lambda c: c.start())
-
-    @pl.when(is_owner)
-    def _():
-        pltpu.make_async_copy(
-            hbuf.at[j, pl.ds(pl.multiple_of(mine * R, 8), R)], rbuf.at[chip, j], rs_recv
-        ).start()
-
-    input_part(1, 3)
-
-    @pl.when(is_owner)
-    def _():
-        pltpu.make_async_copy(rbuf, rbuf, rs_recv).wait()
-        total = rbuf[0]
-        for t in range(1, chips):
-            total = total + rbuf[t]
-        sbuf[...] = total * scale
-        ag_each(lambda c: c.start())
-        pltpu.make_async_copy(sbuf, obuf.at[core, mine], ag_recv).start()
-
+    reduce_start(late)
+    input_part(1, 2)
+    share_start(early)
+    input_part(2, 3)
+    gather_start(late)
     input_part(3, 4)
-    pltpu.make_async_copy(obuf.at[core], obuf.at[core], ag_recv).wait()
-    sib_copy().start()
-    sib_copy().wait_recv()
-    blocks = [obuf[:, :, q].reshape(2 * keep, LANES) for q in range(J)]
+    share_start(late)
+    for p in range(J):
+        sib_copy(p).wait_recv()
+    blocks = [obuf[q].reshape(2 * keep, LANES) for q in range(J)]
     for dh in range(3):
         for slot in range(3):
             at = (dh * 3 + slot) * fl
@@ -351,14 +377,15 @@
                 @pl.when(jnp.logical_not(far(d)))
                 def _():
                     space_forward(d, p, 0).wait_send()
-    pair_copy().wait_send()
-    rs_each(lambda c: c.wait_send())
-
-    @pl.when(is_owner)
-    def _():
-        ag_each(lambda c: c.wait_send())
-
-    sib_copy().wait_send()
+    for p in range(J):
+        pair_copy(p).wait_send()
+        rs_each(p, lambda c: c.wait_send())
+
+        @pl.when(is_owner)
+        def _():
+            ag_each(p, lambda c: c.wait_send())
+
+        sib_copy(p).wait_send()
 
 
 def on_device(activations, kernel, preact, upstream):
@@ -394,16 +421,17 @@
             pltpu.VMEM((padded, LANES), jnp.bfloat16),
             pltpu.VMEM((J, 3, 3, fl, LANES), jnp.bfloat16),
             pltpu.VMEM((J, 3, 3, fl, LANES), jnp.bfloat16),
-            pltpu.VMEM((3, LANES, 3 * J * fl), jnp.bfloat16),
+            pltpu.VMEM((LANES, 9 * J * fl), jnp.bfloat16),
             pltpu.VMEM((J, 2 * keep, LANES), jnp.float32),
             pltpu.VMEM((J, keep, LANES), jnp.float32),
             pltpu.VMEM((J, keep, LANES), jnp.float32),
-            pltpu.VMEM((chips, J, R, LANES), jnp.float32),
+            pltpu.VMEM((J, chips, R, LANES), jnp.float32),
             pltpu.VMEM((J, R, LANES), jnp.float32),
-            pltpu.VMEM((2, owners, J, R, LANES), jnp.float32),
+            pltpu.VMEM((J, 2, owners, R, LANES), jnp.float32),
             dma((3, J, 2)), dma((2, 2)), dma((peers, 2)), dma((2, peers, 2)),
             dma((2, peers)), dma((peers,)), dma((J,)),
-            dma, dma, dma((J, owners)), dma, dma((chips,)), dma, dma, dma,
+            dma((J,)), dma((J,)), dma((J, owners)), dma((J,)), dma((J, chips)), dma((J,)),
+            dma((J,)), dma((J,)),
         ],
         compiler_params=pltpu.CompilerParams(
             collective_id=0, has_side_effects=True, vmem_limit_bytes=40 * 2**20

time: 42.5 us -> 41.7 us (0.981)
  Pallas kernels: 37.9 us -> 37.1 us
    pallas_call x1, Pallas kernels: 37.9 us -> 37.1 us  [on_device(): pl.pallas_call(functools.partial(kernel_body, dims), out_shape=(jax.Shape...]
where the time goes in v4:
time: 41.7 us; the launch traced here: 41.5 us
  Pallas kernels  37.1 us (89%)
  local copies, waits for them, and re-layouts  2.54 us (6%)
  other arithmetic  1.26 us (3%)
  between operations  0.66 us (2%)
    pallas_call x1, Pallas kernels, on_device(): pl.pallas_call(functools.partial(kernel_body, dims), out_shape=(jax.Shape...  37.1 us
    unnamed x6, local copies, waits for them, and re-layouts  2.45 us
    select_n x1, other arithmetic, on_device(): jnp.where(preact > 0, upstream, jnp.zeros_like(upstream)).reshape(fl, cells)  1.26 us

profile of v4, /device:TPU:1, one launch (start us, length us, event | category | flops | bytes accessed | tf_op | source)
XLA Modules:
  0.0 41.5 jit_solution(86585631656763663)
XLA Ops:
  0.6 0.0 copy-start.1
  0.6 1.3 %compare_select_fusion = bf16[32,1,56,128]{3,2,1,0:T(8,128)(2,1)S(1)} fusion(bf16[32,1,56,128]{3,2,1,0:T(8,128)(2,1)} %param.7, bf16[32,1,56,128]{3,2,1,0:T(8,128)(2,1)} %param.6), kind=kLoop, calls=%fused_computation | loop fusion | flops 458752 | bytes 1376256 | tf_op jit(solution)/shard_map/jit(_where)/select_n | solution.py:398
  1.9 0.0 copy-done.1
  1.9 0.0 copy-start
  1.9 0.1 copy_bitcast_fusion
  2.0 0.8 %copy-done = bf16[32,64,3,3,3]{1,0,4,3,2:T(8,128)(2,1)S(1)} copy-done((bf16[32,64,3,3,3]{1,0,4,3,2:T(8,128)(2,1)S(1)}, bf16[32,64,3,3,3]{1,0,4,3,2:T(8,128)(2,1)}, u32[]{:S(2)}) %copy-start) | copy-done | bytes 110616
  2.9 37.1 %shard_map.59 = (bf16[32,7168]{1,0:T(8,128)(2,1)S(1)}, f32[27,32,64]{2,1,0:T(8,128)S(1)}) custom-call(bf16[32,7168]{1,0:T(8,128)(2,1)S(1)} %get-tuple-element.9.m_ref, bf16[32,7168]{1,0:T(8,128)(2,1)S(1)} %get-tuple-element.8.a_ref, bf16[27,32,64]{2,1,0:T(8,128)(2,1)S(1)} %bitcast.22), custom_call_target="tpu_custom_call" | custom-call | tf_op jit(solution)/shard_map/pallas_call | solution.py:411
  39.9 0.8 %copy.9 = bf16[4,8,56,128]{3,2,1,0:T(8,128)(2,1)} copy(bf16[4,8,56,128]{3,1,2,0:T(8,128)(2,1)S(1)} %bitcast.20) | data formatting | bytes 917504
  40.8 0.8 %copy.13 = f32[32,64,3,3,3]{1,0,4,3,2:T(8,128)} copy(f32[32,64,3,3,3]{1,0,4,3,2:T(8,128)S(1)} %bitcast.21) | data formatting | bytes 442368
Async XLA Ops:
  0.6 1.3 %copy-start.1 = (bf16[32,1,56,128]{3,2,1,0:T(8,128)(2,1)S(1)}, bf16[32,1,56,128]{3,2,1,0:T(8,128)(2,1)}, u32[]{:S(2)}) copy-start(bf16[32,1,56,128]{3,2,1,0:T(8,128)(2,1)} %param.4) | copy-start | bytes 1376260
  1.9 0.9 %copy-start = (bf16[32,64,3,3,3]{1,0,4,3,2:T(8,128)(2,1)S(1)}, bf16[32,64,3,3,3]{1,0,4,3,2:T(8,128)(2,1)}, u32[]{:S(2)}) copy-start(bf16[32,64,3,3,3]{1,0,4,3,2:T(8,128)(2,1)} %param.5) | copy-start | bytes 331780

commit v5 on v4

--- a/solution.py
+++ b/solution.py
@@ -59,19 +59,6 @@
             device_id_type=MESH,
         )
 
-    edge = jnp.zeros((3, J, fl, LANES), jnp.bfloat16)
-    mbuf[:, :, :, :LANES] = edge
-    mbuf[:, :, :, LANES + cells :] = edge
-    mbuf[1, j, :, LANES : LANES + cells] = m_ref[...]
-
-    @pl.when(s == 0)
-    def _():
-        mbuf[0, :, :, LANES : LANES + cells] = jnp.zeros((J, fl, cells), jnp.bfloat16)
-
-    @pl.when(s == S - 1)
-    def _():
-        mbuf[2, :, :, LANES : LANES + cells] = jnp.zeros((J, fl, cells), jnp.bfloat16)
-
     next_to = (s > 0).astype(jnp.int32) + (s < S - 1).astype(jnp.int32)
     pl.semaphore_wait(barrier, chips * J - 1 + next_to)
 
@@ -96,11 +83,21 @@
             device_id={"space": s, "filt": peer(p)}, device_id_type=MESH,
         )
 
+    def own_copy(part, to_slot, space, filt, send):
+        return pltpu.make_async_remote_copy(
+            src_ref=m_ref.at[:, (pl.ds(0, half), pl.ds(half, cells - half))[part]],
+            dst_ref=mbuf.at[to_slot, j, :, parts[part]],
+            send_sem=send,
+            recv_sem=m_recv.at[to_slot, j, part],
+            device_id={"space": space, "filt": filt},
+            device_id_type=MESH,
+        )
+
     def space_copy(d, part):
-        return slab_copy(1, j, part, 1 - d, s + d, j, sp_send.at[(d + 1) // 2, part])
+        return own_copy(part, 1 - d, s + d, j, sp_send.at[(d + 1) // 2, part])
 
     def filt_copy(p, part):
-        return slab_copy(1, j, part, 1, s, peer(p), fl_send.at[p - 1, part])
+        return own_copy(part, 1, s, peer(p), fl_send.at[p - 1, part])
 
     def space_forward(d, p, part):
         return slab_copy(
@@ -117,22 +114,39 @@
             @pl.when(valid(d))
             def _():
                 space_copy(d, first).start()
+
+    edge = jnp.zeros((3, J, fl, LANES), jnp.bfloat16)
+    mbuf[:, :, :, :LANES] = edge
+    mbuf[:, :, :, LANES + cells :] = edge
+    mbuf[1, j, :, LANES : LANES + cells] = m_ref[...]
+
+    @pl.when(s == 0)
+    def _():
+        mbuf[0, :, :, LANES : LANES + cells] = jnp.zeros((J, fl, cells), jnp.bfloat16)
+
+    @pl.when(s == S - 1)
+    def _():
+        mbuf[2, :, :, LANES : LANES + cells] = jnp.zeros((J, fl, cells), jnp.bfloat16)
 
     abuf[:LANES] = jnp.zeros((LANES, LANES), jnp.bfloat16)
     abuf[LANES + cells :] = jnp.zeros((LANES, LANES), jnp.bfloat16)
     gbuf[...] = jnp.zeros_like(gbuf)
     column = lax.broadcasted_iota(jnp.int32, (cl, LANES), 1)
 
-    @pl.loop(0, H)
-    def _(row):
-        base = pl.multiple_of(row * LANES, LANES)
-        x = a_ref[:, pl.ds(base, LANES)].astype(jnp.float32)
-        left = jnp.where(column == 0, 0.0, pltpu.roll(x, 1, 1))
-        right = jnp.where(column == LANES - 1, 0.0, pltpu.roll(x, LANES - 1, 1))
+    group = 8 if H % 8 == 0 else 1
+
+    @pl.loop(0, H // group)
+    def _(i):
+        base = pl.multiple_of(i * group * LANES, LANES)
+        wide_x = a_ref[:, pl.ds(base, group * LANES)].astype(jnp.float32)
         rest = jnp.zeros((LANES - 3 * cl, LANES), jnp.float32)
-        stacked = jnp.concatenate([left, x, right, rest], axis=0)
-        to = pl.ds(pl.multiple_of(row * LANES + LANES, LANES), LANES)
-        abuf[to, :] = stacked.T.astype(jnp.bfloat16)
+        for row in range(group):
+            x = wide_x[:, row * LANES : (row + 1) * LANES]
+            left = jnp.where(column == 0, 0.0, pltpu.roll(x, 1, 1))
+            right = jnp.where(column == LANES - 1, 0.0, pltpu.roll(x, LANES - 1, 1))
+            stacked = jnp.concatenate([left, x, right, rest], axis=0)
+            to = pl.ds(pl.multiple_of(base + (row + 1) * LANES, LANES), LANES)
+            abuf[to, :] = stacked.T.astype(jnp.bfloat16)
 
     for q in range(J):
         for dh in range(3):

time: 41.7 us -> 43 us (1.031)
  Pallas kernels: 37.1 us -> 38.4 us
    pallas_call x1, Pallas kernels: 37.1 us -> 38.4 us  [on_device(): pl.pallas_call(functools.partial(kernel_body, dims), out_shape=(jax.Shape...]
where the time goes in v5:
time: 43 us; the launch traced here: 42.8 us
  Pallas kernels  38.4 us (89%)
  local copies, waits for them, and re-layouts  2.54 us (6%)
  other arithmetic  1.26 us (3%)
  between operations  0.66 us (2%)
    pallas_call x1, Pallas kernels, on_device(): pl.pallas_call(functools.partial(kernel_body, dims), out_shape=(jax.Shape...  38.4 us
    unnamed x6, local copies, waits for them, and re-layouts  2.45 us
    select_n x1, other arithmetic, on_device(): jnp.where(preact > 0, upstream, jnp.zeros_like(upstream)).reshape(fl, cells)  1.26 us

profile of v5, /device:TPU:1, one launch (start us, length us, event | category | flops | bytes accessed | tf_op | source)
XLA Modules:
  0.0 42.8 jit_solution(16576374846537108658)
XLA Ops:
  0.6 0.0 copy-start.1
  0.6 1.3 %compare_select_fusion = bf16[32,1,56,128]{3,2,1,0:T(8,128)(2,1)S(1)} fusion(bf16[32,1,56,128]{3,2,1,0:T(8,128)(2,1)} %param.7, bf16[32,1,56,128]{3,2,1,0:T(8,128)(2,1)} %param.6), kind=kLoop, calls=%fused_computation | loop fusion | flops 458752 | bytes 1376256 | tf_op jit(solution)/shard_map/jit(_where)/select_n | solution.py:412
  1.9 0.0 copy-done.1
  1.9 0.0 copy-start
  1.9 0.1 copy_bitcast_fusion
  2.0 0.8 %copy-done = bf16[32,64,3,3,3]{1,0,4,3,2:T(8,128)(2,1)S(1)} copy-done((bf16[32,64,3,3,3]{1,0,4,3,2:T(8,128)(2,1)S(1)}, bf16[32,64,3,3,3]{1,0,4,3,2:T(8,128)(2,1)}, u32[]{:S(2)}) %copy-start) | copy-done | bytes 110616
  2.9 38.4 %shard_map.59 = (bf16[32,7168]{1,0:T(8,128)(2,1)S(1)}, f32[27,32,64]{2,1,0:T(8,128)S(1)}) custom-call(bf16[32,7168]{1,0:T(8,128)(2,1)S(1)} %get-tuple-element.9.m_ref, bf16[32,7168]{1,0:T(8,128)(2,1)S(1)} %get-tuple-element.8.a_ref, bf16[27,32,64]{2,1,0:T(8,128)(2,1)S(1)} %bitcast.22), custom_call_target="tpu_custom_call" | custom-call | tf_op jit(solution)/shard_map/pallas_call | solution.py:425
  41.2 0.8 %copy.9 = bf16[4,8,56,128]{3,2,1,0:T(8,128)(2,1)} copy(bf16[4,8,56,128]{3,1,2,0:T(8,128)(2,1)S(1)} %bitcast.20) | data formatting | bytes 917504
  42.1 0.8 %copy.13 = f32[32,64,3,3,3]{1,0,4,3,2:T(8,128)} copy(f32[32,64,3,3,3]{1,0,4,3,2:T(8,128)S(1)} %bitcast.21) | data formatting | bytes 442368
Async XLA Ops:
  0.6 1.3 %copy-start.1 = (bf16[32,1,56,128]{3,2,1,0:T(8,128)(2,1)S(1)}, bf16[32,1,56,128]{3,2,1,0:T(8,128)(2,1)}, u32[]{:S(2)}) copy-start(bf16[32,1,56,128]{3,2,1,0:T(8,128)(2,1)} %param.4) | copy-start | bytes 1376260
  1.9 0.9 %copy-start = (bf16[32,64,3,3,3]{1,0,4,3,2:T(8,128)(2,1)S(1)}, bf16[32,64,3,3,3]{1,0,4,3,2:T(8,128)(2,1)}, u32[]{:S(2)}) copy-start(bf16[32,64,3,3,3]{1,0,4,3,2:T(8,128)(2,1)} %param.5) | copy-start | bytes 331780

commit v6 on v4

--- a/solution.py
+++ b/solution.py
@@ -13,7 +13,7 @@
 
 def kernel_body(
     dims, m_ref, a_ref, k_ref, ig_ref, kg_ref,
-    mbuf, abuf, kpart, kbuf, ktr, gbuf, pbuf, hbuf, rbuf, sbuf, obuf,
+    mbuf, abuf, kpart, kbuf, kown, kother, ybuf, gbuf, pbuf, hbuf, rbuf, sbuf, obuf,
     m_recv, sp_send, fl_send, spf_send, flf_send, k_send, k_recv,
     pair_send, pair_recv, rs_send, rs_recv, ag_send, ag_recv, sib_send, sib_recv,
 ):
@@ -30,7 +30,6 @@
     half = (H // 2) * LANES
     cells = H * LANES
     parts = (pl.ds(LANES, half), pl.ds(LANES + half, cells - half))
-    k3 = 3 * J * fl
     cl = a_ref.shape[0]
 
     def valid(d):
@@ -147,7 +146,6 @@
                 kpart[q, dh, slot] = jnp.concatenate(taps, axis=1).astype(jnp.bfloat16)
     for p in range(1, J):
         k_copy(p).start()
-    kbuf[j] = kpart[j]
 
     def weight_terms(pieces, part):
         rows = H // 4
@@ -290,14 +288,59 @@
     weight_terms(own_all, 1)
     pair_start(early)
 
+    def taps_of(blocks):
+        return jnp.concatenate(blocks, axis=0).astype(jnp.float32).T.astype(jnp.bfloat16)
+
+    kown[...] = taps_of([kpart[j, dh, slot] for dh in range(3) for slot in range(3)])
+    reduce_start(early)
+
+    rows = H // 8
+    wide = rows * LANES
+    cols = lax.rem(lax.broadcasted_iota(jnp.int32, (cl, wide), 1), LANES)
+
+    def slabs_at(at, pieces):
+        return jnp.concatenate(
+            [
+                mbuf[slot, q, :, pl.ds(pl.multiple_of((at + 2 - dh) * LANES, LANES), wide)]
+                for dh in range(3)
+                for slot, q in pieces
+            ],
+            axis=0,
+        )
+
+    @pl.loop(0, 4)
+    def _(i):
+        for sub in range(2):
+            at = (2 * i + sub) * rows
+            ybuf[:, pl.ds(pl.multiple_of(at * LANES, LANES), wide)] = jnp.dot(
+                kown[: 3 * cl], slabs_at(at, own_all), preferred_element_type=jnp.float32
+            )
+
+    def input_part(first_step, last_step):
+        @pl.loop(first_step, last_step)
+        def _(i):
+            for sub in range(2):
+                at = (2 * i + sub) * rows
+                to = pl.ds(pl.multiple_of(at * LANES, LANES), wide)
+                total = ybuf[:, to]
+                if J > 1:
+                    total = total + jnp.dot(
+                        kother[: 3 * cl], slabs_at(at, other_all),
+                        preferred_element_type=jnp.float32,
+                    )
+                first = pltpu.roll(total[:cl], wide - 1, 1)
+                last = pltpu.roll(total[2 * cl :], 1, 1)
+                result = total[cl : 2 * cl] + jnp.where(cols == LANES - 1, 0.0, first)
+                result = result + jnp.where(cols == 0, 0.0, last)
+                ig_ref[:, to] = result.astype(jnp.bfloat16)
+
     for p in range(1, J):
         got = kbuf.at[peer(p)]
         pltpu.make_async_copy(got, got, k_recv.at[peer(p)]).wait()
-    stacked = jnp.concatenate(
-        [kbuf[q, dh, slot] for dh in range(3) for slot in range(3) for q in range(J)], axis=0
-    )
-    ktr[...] = stacked.astype(jnp.float32).T.astype(jnp.bfloat16)
-    reduce_start(early)
+    if J > 1:
+        kother[...] = taps_of(
+            [kbuf[q, dh, slot] for dh in range(3) for slot, q in other_all]
+        )
 
     for part in (1, 0):
         for d in (-1, 1):
@@ -310,32 +353,6 @@
         if part == 1:
             gather_start(early)
     pair_start(late)
-
-    rows = H // 8
-    wide = rows * LANES
-    cols = lax.rem(lax.broadcasted_iota(jnp.int32, (cl, wide), 1), LANES)
-
-    def input_part(first_step, last_step):
-        @pl.loop(first_step, last_step)
-        def _(i):
-            for sub in range(2):
-                at = (2 * i + sub) * rows
-                slabs = [
-                    mbuf[
-                        :, :, :, pl.ds(pl.multiple_of((at + 2 - dh) * LANES, LANES), wide)
-                    ].reshape(k3, wide)
-                    for dh in range(3)
-                ]
-                total = jnp.dot(
-                    ktr[: 3 * cl], jnp.concatenate(slabs, axis=0),
-                    preferred_element_type=jnp.float32,
-                )
-                first = pltpu.roll(total[:cl], wide - 1, 1)
-                last = pltpu.roll(total[2 * cl :], 1, 1)
-                result = total[cl : 2 * cl] + jnp.where(cols == LANES - 1, 0.0, first)
-                result = result + jnp.where(cols == 0, 0.0, last)
-                to = pl.ds(pl.multiple_of(at * LANES, LANES), wide)
-                ig_ref[:, to] = result.astype(jnp.bfloat16)
 
     input_part(0, 1)
     reduce_start(late)
@@ -421,7 +438,9 @@
             pltpu.VMEM((padded, LANES), jnp.bfloat16),
             pltpu.VMEM((J, 3, 3, fl, LANES), jnp.bfloat16),
             pltpu.VMEM((J, 3, 3, fl, LANES), jnp.bfloat16),
-            pltpu.VMEM((LANES, 9 * J * fl), jnp.bfloat16),
+            pltpu.VMEM((LANES, 9 * fl), jnp.bfloat16),
+            pltpu.VMEM((LANES, 9 * peers * fl), jnp.bfloat16),
+            pltpu.VMEM((3 * cl, cells), jnp.float32),
             pltpu.VMEM((J, 2 * keep, LANES), jnp.float32),
             pltpu.VMEM((J, keep, LANES), jnp.float32),
             pltpu.VMEM((J, keep, LANES), jnp.float32),

time: 41.7 us -> 42.7 us (1.024)
  Pallas kernels: 37.1 us -> 38.1 us
    pallas_call x1, Pallas kernels: 37.1 us -> 38.1 us  [on_device(): pl.pallas_call(functools.partial(kernel_body, dims), out_shape=(jax.Shape...]
where the time goes in v6:
time: 42.7 us; the launch traced here: 42.5 us
  Pallas kernels  38.1 us (89%)
  local copies, waits for them, and re-layouts  2.54 us (6%)
  other arithmetic  1.26 us (3%)
  between operations  0.66 us (2%)
    pallas_call x1, Pallas kernels, on_device(): pl.pallas_call(functools.partial(kernel_body, dims), out_shape=(jax.Shape...  38.1 us
    unnamed x6, local copies, waits for them, and re-layouts  2.45 us
    select_n x1, other arithmetic, on_device(): jnp.where(preact > 0, upstream, jnp.zeros_like(upstream)).reshape(fl, cells)  1.26 us

profile of v6, /device:TPU:1, one launch (start us, length us, event | category | flops | bytes accessed | tf_op | source)
XLA Modules:
  0.0 42.5 jit_solution(2344069334034440729)
XLA Ops:
  0.6 0.0 copy-start.1
  0.6 1.3 %compare_select_fusion = bf16[32,1,56,128]{3,2,1,0:T(8,128)(2,1)S(1)} fusion(bf16[32,1,56,128]{3,2,1,0:T(8,128)(2,1)} %param.7, bf16[32,1,56,128]{3,2,1,0:T(8,128)(2,1)} %param.6), kind=kLoop, calls=%fused_computation | loop fusion | flops 458752 | bytes 1376256 | tf_op jit(solution)/shard_map/jit(_where)/select_n | solution.py:415
  1.9 0.0 copy-done.1
  1.9 0.0 copy-start
  1.9 0.1 copy_bitcast_fusion
  2.0 0.8 %copy-done = bf16[32,64,3,3,3]{1,0,4,3,2:T(8,128)(2,1)S(1)} copy-done((bf16[32,64,3,3,3]{1,0,4,3,2:T(8,128)(2,1)S(1)}, bf16[32,64,3,3,3]{1,0,4,3,2:T(8,128)(2,1)}, u32[]{:S(2)}) %copy-start) | copy-done | bytes 110616
  2.9 38.1 %shard_map.59 = (bf16[32,7168]{1,0:T(8,128)(2,1)S(1)}, f32[27,32,64]{2,1,0:T(8,128)S(1)}) custom-call(bf16[32,7168]{1,0:T(8,128)(2,1)S(1)} %get-tuple-element.9.m_ref, bf16[32,7168]{1,0:T(8,128)(2,1)S(1)} %get-tuple-element.8.a_ref, bf16[27,32,64]{2,1,0:T(8,128)(2,1)S(1)} %bitcast.22), custom_call_target="tpu_custom_call" | custom-call | tf_op jit(solution)/shard_map/pallas_call | solution.py:428
  40.9 0.8 %copy.9 = bf16[4,8,56,128]{3,2,1,0:T(8,128)(2,1)} copy(bf16[4,8,56,128]{3,1,2,0:T(8,128)(2,1)S(1)} %bitcast.20) | data formatting | bytes 917504
  41.8 0.8 %copy.13 = f32[32,64,3,3,3]{1,0,4,3,2:T(8,128)} copy(f32[32,64,3,3,3]{1,0,4,3,2:T(8,128)S(1)} %bitcast.21) | data formatting | bytes 442368
Async XLA Ops:
  0.6 1.3 %copy-start.1 = (bf16[32,1,56,128]{3,2,1,0:T(8,128)(2,1)S(1)}, bf16[32,1,56,128]{3,2,1,0:T(8,128)(2,1)}, u32[]{:S(2)}) copy-start(bf16[32,1,56,128]{3,2,1,0:T(8,128)(2,1)} %param.4) | copy-start | bytes 1376260
  1.9 0.9 %copy-start = (bf16[32,64,3,3,3]{1,0,4,3,2:T(8,128)(2,1)S(1)}, bf16[32,64,3,3,3]{1,0,4,3,2:T(8,128)(2,1)}, u32[]{:S(2)}) copy-start(bf16[32,64,3,3,3]{1,0,4,3,2:T(8,128)(2,1)} %param.5) | copy-start | bytes 331780

commit v7 on v4

--- a/solution.py
+++ b/solution.py
@@ -307,8 +307,6 @@
                     arrived(1 + d, peer(p), part)
         if J > 1:
             weight_terms(other_all, part)
-        if part == 1:
-            gather_start(early)
     pair_start(late)
 
     rows = H // 8
@@ -337,12 +335,12 @@
                 to = pl.ds(pl.multiple_of(at * LANES, LANES), wide)
                 ig_ref[:, to] = result.astype(jnp.bfloat16)
 
+    gather_start(early)
     input_part(0, 1)
     reduce_start(late)
-    input_part(1, 2)
+    input_part(1, 3)
+    gather_start(late)
     share_start(early)
-    input_part(2, 3)
-    gather_start(late)
     input_part(3, 4)
     share_start(late)
     for p in range(J):

time: 41.7 us -> 41.5 us (level)
  no operation moved by 1% of the time
where the time goes in v7:
time: 41.5 us; the launch traced here: 41.4 us
  Pallas kernels  36.9 us (89%)
  local copies, waits for them, and re-layouts  2.54 us (6%)
  other arithmetic  1.26 us (3%)
  between operations  0.66 us (2%)
    pallas_call x1, Pallas kernels, on_device(): pl.pallas_call(functools.partial(kernel_body, dims), out_shape=(jax.Shape...  36.9 us
    unnamed x6, local copies, waits for them, and re-layouts  2.45 us
    select_n x1, other arithmetic, on_device(): jnp.where(preact > 0, upstream, jnp.zeros_like(upstream)).reshape(fl, cells)  1.26 us

profile of v7, /device:TPU:1, one launch (start us, length us, event | category | flops | bytes accessed | tf_op | source)
XLA Modules:
  0.0 41.4 jit_solution(1163735587178582530)
XLA Ops:
  0.6 0.0 copy-start.1
  0.6 1.3 %compare_select_fusion = bf16[32,1,56,128]{3,2,1,0:T(8,128)(2,1)S(1)} fusion(bf16[32,1,56,128]{3,2,1,0:T(8,128)(2,1)} %param.7, bf16[32,1,56,128]{3,2,1,0:T(8,128)(2,1)} %param.6), kind=kLoop, calls=%fused_computation | loop fusion | flops 458752 | bytes 1376256 | tf_op jit(solution)/shard_map/jit(_where)/select_n | solution.py:396
  1.9 0.0 copy-done.1
  1.9 0.0 copy-start
  1.9 0.1 copy_bitcast_fusion
  2.0 0.8 %copy-done = bf16[32,64,3,3,3]{1,0,4,3,2:T(8,128)(2,1)S(1)} copy-done((bf16[32,64,3,3,3]{1,0,4,3,2:T(8,128)(2,1)S(1)}, bf16[32,64,3,3,3]{1,0,4,3,2:T(8,128)(2,1)}, u32[]{:S(2)}) %copy-start) | copy-done | bytes 110616
  2.9 36.9 %shard_map.59 = (bf16[32,7168]{1,0:T(8,128)(2,1)S(1)}, f32[27,32,64]{2,1,0:T(8,128)S(1)}) custom-call(bf16[32,7168]{1,0:T(8,128)(2,1)S(1)} %get-tuple-element.9.m_ref, bf16[32,7168]{1,0:T(8,128)(2,1)S(1)} %get-tuple-element.8.a_ref, bf16[27,32,64]{2,1,0:T(8,128)(2,1)S(1)} %bitcast.22), custom_call_target="tpu_custom_call" | custom-call | tf_op jit(solution)/shard_map/pallas_call | solution.py:409
  39.8 0.8 %copy.9 = bf16[4,8,56,128]{3,2,1,0:T(8,128)(2,1)} copy(bf16[4,8,56,128]{3,1,2,0:T(8,128)(2,1)S(1)} %bitcast.20) | data formatting | bytes 917504
  40.6 0.8 %copy.13 = f32[32,64,3,3,3]{1,0,4,3,2:T(8,128)} copy(f32[32,64,3,3,3]{1,0,4,3,2:T(8,128)S(1)} %bitcast.21) | data formatting | bytes 442368
Async XLA Ops:
  0.6 1.3 %copy-start.1 = (bf16[32,1,56,128]{3,2,1,0:T(8,128)(2,1)S(1)}, bf16[32,1,56,128]{3,2,1,0:T(8,128)(2,1)}, u32[]{:S(2)}) copy-start(bf16[32,1,56,128]{3,2,1,0:T(8,128)(2,1)} %param.4) | copy-start | bytes 1376260
  1.9 0.9 %copy-start = (bf16[32,64,3,3,3]{1,0,4,3,2:T(8,128)(2,1)S(1)}, bf16[32,64,3,3,3]{1,0,4,3,2:T(8,128)(2,1)}, u32[]{:S(2)}) copy-start(bf16[32,64,3,3,3]{1,0,4,3,2:T(8,128)(2,1)} %param.5) | copy-start | bytes 331780

commit v8 on v7

--- a/solution.py
+++ b/solution.py
@@ -13,8 +13,8 @@
 
 def kernel_body(
     dims, m_ref, a_ref, k_ref, ig_ref, kg_ref,
-    mbuf, abuf, kpart, kbuf, ktr, gbuf, pbuf, hbuf, rbuf, sbuf, obuf,
-    m_recv, sp_send, fl_send, spf_send, flf_send, k_send, k_recv,
+    kraw, mbuf, abuf, kpart, kbuf, ktr, gbuf, pbuf, hbuf, rbuf, sbuf, obuf,
+    k_in, m_recv, sp_send, fl_send, spf_send, flf_send, k_send, k_recv,
     pair_send, pair_recv, rs_send, rs_recv, ag_send, ag_recv, sib_send, sib_recv,
 ):
     S, J, fl, H, R, owners, scale = dims
@@ -42,6 +42,8 @@
     def peer(p):
         return lax.rem(j + p, J)
 
+    load = pltpu.make_async_copy(k_ref, kraw, k_in)
+    load.start()
     barrier = pltpu.get_barrier_semaphore()
     for d in (-1, 1):
         @pl.when(valid(d))
@@ -134,11 +136,13 @@
         to = pl.ds(pl.multiple_of(row * LANES + LANES, LANES), LANES)
         abuf[to, :] = stacked.T.astype(jnp.bfloat16)
 
+    load.wait()
+
     for q in range(J):
         for dh in range(3):
             for slot in range(3):
                 taps = [
-                    k_ref[(2 - slot) * 9 + dh * 3 + dw].astype(jnp.float32)[
+                    kraw[(2 - slot) * 9 + dh * 3 + dw].astype(jnp.float32)[
                         :, q * cl : (q + 1) * cl
                     ]
                     for dw in range(3)
@@ -412,9 +416,10 @@
             jax.ShapeDtypeStruct((cl, cells), jnp.bfloat16),
             jax.ShapeDtypeStruct((27, fl, J * cl), jnp.float32),
         ),
-        in_specs=[vmem] * 3,
+        in_specs=[vmem, vmem, pl.BlockSpec(memory_space=pltpu.HBM)],
         out_specs=(vmem, vmem),
         scratch_shapes=[
+            pltpu.VMEM((27, fl, J * cl), jnp.bfloat16),
             pltpu.VMEM((3, J, fl, padded), jnp.bfloat16),
             pltpu.VMEM((padded, LANES), jnp.bfloat16),
             pltpu.VMEM((J, 3, 3, fl, LANES), jnp.bfloat16),
@@ -426,13 +431,13 @@
             pltpu.VMEM((J, chips, R, LANES), jnp.float32),
             pltpu.VMEM((J, R, LANES), jnp.float32),
             pltpu.VMEM((J, 2, owners, R, LANES), jnp.float32),
-            dma((3, J, 2)), dma((2, 2)), dma((peers, 2)), dma((2, peers, 2)),
+            dma, dma((3, J, 2)), dma((2, 2)), dma((peers, 2)), dma((2, peers, 2)),
             dma((2, peers)), dma((peers,)), dma((J,)),
             dma((J,)), dma((J,)), dma((J, owners)), dma((J,)), dma((J, chips)), dma((J,)),
             dma((J,)), dma((J,)),
         ],
         compiler_params=pltpu.CompilerParams(
-            collective_id=0, has_side_effects=True, vmem_limit_bytes=40 * 2**20
+            collective_id=0, has_side_effects=True, vmem_limit_bytes=62 * 2**20
         ),
     )(masked, acts, taps)
     input_grad = ig.reshape(cl, depth, H, W)

time: 41.5 us -> 44.8 us (1.080)
  Pallas kernels: 36.9 us -> 39 us
  local copies, waits for them, and re-layouts: 2.54 us -> 3.7 us
    pallas_call x1, Pallas kernels: 36.9 us -> 39 us  [on_device(): pl.pallas_call(functools.partial(kernel_body, dims), out_shape=(jax.Shape...]
    reshape x1, local copies, waits for them, and re-layouts: 0.09 us -> 1.01 us  [on_device(): acts = activations.reshape(cl, cells)]
where the time goes in v8:
time: 44.8 us; the launch traced here: 44.6 us
  Pallas kernels  39 us (87%)
  local copies, waits for them, and re-layouts  3.7 us (8%)
  other arithmetic  1.26 us (3%)
  between operations  0.66 us (1%)
    pallas_call x1, Pallas kernels, on_device(): pl.pallas_call(functools.partial(kernel_body, dims), out_shape=(jax.Shape...  39 us
    unnamed x6, local copies, waits for them, and re-layouts  2.69 us
    select_n x1, other arithmetic, on_device(): jnp.where(preact > 0, upstream, jnp.zeros_like(upstream)).reshape(fl, cells)  1.26 us
    reshape x1, local copies, waits for them, and re-layouts, on_device(): acts = activations.reshape(cl, cells)  1.01 us

profile of v8, /device:TPU:1, one launch (start us, length us, event | category | flops | bytes accessed | tf_op | source)
XLA Modules:
  0.0 44.6 jit_solution(2313793126514401185)
XLA Ops:
  0.6 0.0 copy-start
  0.6 1.3 %compare_select_fusion = bf16[32,1,56,128]{3,2,1,0:T(8,128)(2,1)S(1)} fusion(bf16[32,1,56,128]{3,2,1,0:T(8,128)(2,1)} %param.7, bf16[32,1,56,128]{3,2,1,0:T(8,128)(2,1)} %param.6), kind=kLoop, calls=%fused_computation | loop fusion | flops 458752 | bytes 1376256 | tf_op jit(solution)/shard_map/jit(_where)/select_n | solution.py:400
  1.9 0.0 copy-done
  1.9 1.0 %copy_bitcast_fusion = (bf16[32,7168]{1,0:T(8,128)(2,1)}, bf16[32,7168]{1,0:T(8,128)(2,1)}) fusion(bf16[4,8,56,128]{3,2,1,0:T(8,128)(2,1)S(1)} %bitcast.21, bf16[4,8,56,128]{3,2,1,0:T(8,128)(2,1)S(1)} %bitcast.20), kind=kLoop, calls=%fused_computation.1 | loop fusion | bytes 1835008 | tf_op jit(solution)/shard_map/reshape | solution.py:401
  2.9 39.0 %shard_map.59 = (bf16[32,7168]{1,0:T(8,128)(2,1)}, f32[27,32,64]{2,1,0:T(8,128)}) custom-call(bf16[32,7168]{1,0:T(8,128)(2,1)} %get-tuple-element.9.m_ref, bf16[32,7168]{1,0:T(8,128)(2,1)} %get-tuple-element.8.a_ref, bf16[27,32,64]{2,1,0:T(8,128)(2,1)} %bitcast.25), custom_call_target="tpu_custom_call" | custom-call | tf_op jit(solution)/shard_map/pallas_call | solution.py:413
  42.0 0.0 copy-start.1
  42.0 1.9 %copy.9 = bf16[4,8,56,128]{3,2,1,0:T(8,128)(2,1)} copy(bf16[4,8,56,128]{3,1,2,0:T(8,128)(2,1)} %bitcast.23) | data formatting | bytes 917504
  43.9 0.0 copy-done.1
  43.9 0.8 %copy.13 = f32[32,64,3,3,3]{1,0,4,3,2:T(8,128)} copy(f32[32,64,3,3,3]{1,0,4,3,2:T(8,128)S(1)} %bitcast.24) | data formatting | bytes 442368
Async XLA Ops:
  0.6 1.3 %copy-start = (bf16[32,1,56,128]{3,2,1,0:T(8,128)(2,1)S(1)}, bf16[32,1,56,128]{3,2,1,0:T(8,128)(2,1)}, u32[]{:S(2)}) copy-start(bf16[32,1,56,128]{3,2,1,0:T(8,128)(2,1)} %param.4) | copy-start | bytes 1376260
  42.0 1.9 %copy-start.1 = (f32[27,32,64]{2,1,0:T(8,128)S(1)}, f32[27,32,64]{2,1,0:T(8,128)}, u32[]{:S(2)}) copy-start(f32[27,32,64]{2,1,0:T(8,128)} %get-tuple-element.5) | copy-start | bytes 663556
